TPU v7x, 32 devices: a whole 2x2x4 slice. The times are simulated.
32 devices in a mesh: seq: 8 (over y, x, core), batch: 4 (over z).
Axes of the slice: x: 2, y: 2, z: 4, core: 2. Of those that a mesh axis runs over, the one named last changes fastest.
Arguments:
- tokens: bfloat16 [4, 3072, 768], P('batch', 'seq'), may hold values from -6 to 6
- segment_ids: int32 [4, 3072], P('batch', 'seq'), may hold values from 0 to 2, as said below
- neighbours: bfloat16 [4, 48, 2, 128, 768], P('batch', 'seq'), may hold values from -6 to 6
- first_gain: float32 [768], replicated, may hold values from 0.5 to 1.5
- first_shift: float32 [768], replicated, may hold values from -1.5 to 1.5
- self_weight: bfloat16 [768, 2304], replicated, may hold values from -0.21875 to 0.21875
- self_output: bfloat16 [768, 768], replicated, may hold values from -0.875 to 0.875
- second_gain: float32 [768], replicated, may hold values from 0.5 to 1.5
- second_shift: float32 [768], replicated, may hold values from -1.5 to 1.5
- query_weight: bfloat16 [768, 768], replicated, may hold values from -0.21875 to 0.21875
- memory_weight: bfloat16 [768, 1536], replicated, may hold values from -0.21875 to 0.21875
- cross_output: bfloat16 [768, 768], replicated, may hold values from -1.75 to 1.75
- third_gain: float32 [768], replicated, may hold values from 0.5 to 1.5
- third_shift: float32 [768], replicated, may hold values from -1.5 to 1.5
- up_weight: bfloat16 [768, 3072], replicated, may hold values from -0.21875 to 0.21875
- down_weight: bfloat16 [3072, 768], replicated, may hold values from -0.109375 to 0.109375
- cotangent: bfloat16 [4, 3072, 768], P('batch', 'seq'), may hold values from -6 to 6
Outputs:
- result: bfloat16 [4, 3072, 768], P('batch', 'seq')
- input_grad: float32 [4, 3072, 768], P('batch', 'seq')
- neighbour_grad: float32 [4, 48, 2, 128, 768], P('batch', 'seq')
- first_gain_grad: float32 [768], P('batch')
- first_shift_grad: float32 [768], P('batch')
- self_weight_grad: float32 [768, 2304], P('batch')
- self_output_grad: float32 [768, 768], P('batch')
- second_gain_grad: float32 [768], P('batch')
- second_shift_grad: float32 [768], P('batch')
- query_weight_grad: float32 [768, 768], P('batch')
- memory_weight_grad: float32 [768, 1536], P('batch')
- cross_output_grad: float32 [768, 768], P('batch')
- third_gain_grad: float32 [768], P('batch')
- third_shift_grad: float32 [768], P('batch')
- up_weight_grad: float32 [768, 3072], P('batch')
- down_weight_grad: float32 [3072, 768], P('batch')
Inputs may be any that keep to these rules, and one draw needn't show every extreme that they name: `segment_ids`: ids never fall along a sequence; each sequence holds three documents: the middle one starts at a position from 1 to 192, the last one at a position from 2880 to 3071.
All inputs are finite; a program needn't handle non-finite values.
Results may differ from a plain program's by a relative error of at most 0.025.
Values may be sent and summed in bfloat16 or wider, within the bound.
A program may use at most 256 MiB of HBM per device.

v0:
```python
import functools
from functools import partial

import jax
import jax.numpy as jnp
from jax import lax
from jax.experimental import pallas as pl
from jax.experimental.pallas import tpu as pltpu
from jax.sharding import PartitionSpec as P
import math

D = 768
HEADS = 12
HEAD = 64
STRETCH = 64
NEIGHBOURS = 2
NEIGHBOUR_LEN = 128
SPAN = NEIGHBOURS * NEIGHBOUR_LEN
EPSILON = 1e-05
NEGATIVE = -1e30
MESH = pl.DeviceIdType.MESH
VM = pltpu.VMEM
F32 = jnp.float32
BF16 = jnp.bfloat16


def matmul(left, right):
    return jnp.dot(left, right, preferred_element_type=F32)


def outer_sum(left, right):
    return lax.dot_general(left, right, (((0,), (0,)), ((), ())), preferred_element_type=F32)


def back_product(left, right):
    return lax.dot_general(left, right, (((1,), (1,)), ((), ())), preferred_element_type=F32)


def low_lanes(shape):
    return lax.broadcasted_iota(jnp.int32, shape, len(shape) - 1) < HEAD


def swap_lanes(values):
    return pltpu.roll(values, HEAD, 1)


def as_row(vector):
    return vector[...].reshape(1, D)


def full_norm(values, gain, shift):
    mean = jnp.mean(values, axis=-1, keepdims=True)
    centred = values - mean
    spread = jnp.mean(centred * centred, axis=-1, keepdims=True)
    return centred * lax.rsqrt(spread + EPSILON) * gain + shift


class Plan:
    def __init__(self, devices, rows):
        self.devices = devices
        self.rows = rows
        self.groups = math.gcd(devices, HEADS)
        self.members = devices // self.groups
        self.slots = HEADS // self.groups

    def place(self):
        me = lax.axis_index("seq")
        return me, lax.div(me, self.members), lax.rem(me, self.members)


def seq_device(index):
    return (index, lax.axis_index("batch"))


def greet(devices):
    barrier = pltpu.get_barrier_semaphore()
    for device in devices:
        pl.semaphore_signal(barrier, inc=1, device_id=device, device_id_type=MESH)
    pl.semaphore_wait(barrier, len(devices))


def send(source, target, send_sem, recv_sem, device):
    return pltpu.make_async_remote_copy(
        src_ref=source,
        dst_ref=target,
        send_sem=send_sem,
        recv_sem=recv_sem,
        device_id=device,
        device_id_type=MESH,
    )


def pack_rows(values, head):
    half = values.shape[0] // 2
    top, bottom = values[:half], values[half:]
    low = low_lanes((half, 2 * HEAD))
    if head % 2 == 0:
        return jnp.where(low, top, swap_lanes(bottom))
    return jnp.where(low, swap_lanes(top), bottom)


def hide(plan, scores, k, g, member, start):
    causal = k == g
    if not (causal or k == 0 or g == plan.groups - 1):
        return scores
    at = lax.broadcasted_iota(jnp.int32, scores.shape, 0)
    allowed = at >= start - k * plan.members * plan.rows
    if causal:
        allowed = allowed & (at <= member * plan.rows + lax.broadcasted_iota(jnp.int32, scores.shape, 1))
    return jnp.where(allowed, scores, NEGATIVE)


def attend_kernel(plan, *refs):
    (
        tokens, gain, shift, segments, far_weight, far_neighbours, far_memory_weight,
        normed, logs, starts, context, edge, far_queries, far_pairs, far_outs, far_memory,
        queries, pairs, outs, memory, weight, neighbours, memory_weight,
        segs, projected, pack_pairs, pack_queries, got_queries, sent_context, got_context,
        pair_send, pair_recv, query_send, query_recv, pass_send, pass_recv,
        back_send, back_recv, seg_send, seg_recv, edge_send, edge_recv, load_sems, memory_sems, store_sems,
    ) = refs
    me, group, member = plan.place()
    devices, groups, members, slots, rows = plan.devices, plan.groups, plan.members, plan.slots, plan.rows
    others = [lax.rem(me + i, devices) for i in range(1, devices)]
    loads = [
        pltpu.make_async_copy(far_weight, weight, load_sems.at[0]),
        pltpu.make_async_copy(far_neighbours, neighbours, load_sems.at[1]),
        pltpu.make_async_copy(far_memory_weight, memory_weight, load_sems.at[2]),
    ]
    for copy in loads:
        copy.start()
    greet([seq_device(o) for o in others])
    half = rows // 2
    stretches = neighbours.shape[0] // SPAN
    low = low_lanes((rows, 2 * HEAD))

    seg_copies = []
    segs[me] = jnp.broadcast_to(segments[...].astype(F32), (8, rows))
    for i, o in enumerate(others):
        copy = send(segs.at[me], segs.at[me], seg_send.at[i], seg_recv.at[me], seq_device(o))
        copy.start()
        seg_copies.append(copy)
    last_rows = pl.ds((stretches - 1) * SPAN, SPAN)
    edge_copy = send(far_neighbours.at[last_rows], edge, edge_send, edge_recv, seq_device(jnp.minimum(me + 1, devices - 1)))

    @pl.when(me < devices - 1)
    def _():
        edge_copy.start()

    normed[...] = full_norm(tokens[...].astype(F32), as_row(gain), as_row(shift)).astype(BF16)

    loads[0].wait()

    @pl.loop(0, 3)
    def _(j):
        columns = pl.ds(pl.multiple_of(j * D, D), D)
        projected[:, columns] = matmul(normed[...], weight[:, columns])

    def pair_copy(slot, away):
        to = lax.rem(group + away, groups)
        return send(
            pack_pairs.at[to * slots + slot], pairs.at[slot, me],
            pair_send.at[slot, away - 1], pair_recv.at[slot, group], seq_device(to * members + member),
        )

    def query_copy(slot, away):
        to = lax.rem(group + away, groups)
        return send(
            pack_queries.at[to * slots + slot], got_queries.at[slot, group],
            query_send.at[slot, away - 1], query_recv.at[slot, group], seq_device(to * members + member),
        )

    def arrived_pair(slot, origin):
        return send(
            pack_pairs.at[0], pairs.at[slot, origin * members + member],
            pair_send.at[slot, 0], pair_recv.at[slot, origin], seq_device(me),
        )

    def arrived_query(slot, origin):
        return send(
            pack_queries.at[0], got_queries.at[slot, origin],
            query_send.at[slot, 0], query_recv.at[slot, origin], seq_device(me),
        )

    def pass_copy(slot, origin, away):
        to = lax.rem(member + away, members)
        place = origin * members + member
        return send(
            pairs.at[slot, place], pairs.at[slot, place],
            pass_send.at[slot, origin, away - 1], pass_recv.at[slot, place], seq_device(group * members + to),
        )

    def passed(slot, origin, away):
        source = lax.rem(member + away, members)
        place = origin * members + source
        return send(
            pairs.at[slot, place], pairs.at[slot, place],
            pass_send.at[slot, origin, 0], pass_recv.at[slot, place], seq_device(me),
        )

    for slot in range(slots):
        for head in range(slot, HEADS, slots):
            block = (head // 2) * 128
            key = projected[:, D + block : D + block + 128]
            value = projected[:, 2 * D + block : 2 * D + block + 128]
            if head % 2 == 0:
                pair = jnp.where(low, key, swap_lanes(value))
            else:
                pair = jnp.where(low, swap_lanes(key), value)
            pack_pairs[head] = pair.astype(BF16)
            query = projected[:, block : block + 128].astype(BF16).astype(F32) * (HEAD ** -0.5)
            pack_queries[head] = pack_rows(query, head).astype(BF16)
        for away in range(1, groups):
            pair_copy(slot, away).start()
            query_copy(slot, away).start()
    for slot in range(slots):
        pairs[slot, me] = pack_pairs[group * slots + slot]
        got_queries[slot, group] = pack_queries[group * slots + slot]
        for away in range(1, members):
            pass_copy(slot, group, away).start()

    for copy in loads[1:]:
        copy.wait()

    def memory_copy(s):
        return pltpu.make_async_copy(memory.at[s], far_memory.at[s], memory_sems.at[s])

    @pl.loop(0, stretches)
    def _(s):
        some = pl.ds(pl.multiple_of(s * SPAN, SPAN), SPAN)
        memory[s + 1] = matmul(neighbours[some], memory_weight[...]).astype(BF16)
        memory_copy(s + 1).start()

    @pl.when(me > 0)
    def _():
        edge_copy.wait_recv()
        memory[0] = matmul(edge[...], memory_weight[...]).astype(BF16)

    @pl.when(me == 0)
    def _():
        memory[0] = jnp.zeros_like(memory[0])
        edge[...] = jnp.zeros_like(edge)

    memory_copy(0).start()

    for copy in seg_copies:
        copy.wait_send()
    for i in range(1, devices):
        source = lax.rem(me + i, devices)
        send(segs.at[source], segs.at[source], seg_send.at[0], seg_recv.at[source], seq_device(me)).wait_recv()

    counts = [
        jnp.sum(jnp.sum((segs[:, 0, :] == value).astype(F32), axis=1, keepdims=True), axis=0, keepdims=True)
        for value in (0.0, 1.0)
    ]
    for g in range(groups):
        mine = segs[g * members + member]
        starts[g] = jnp.where(mine == 0.0, 0.0, counts[0] + jnp.where(mine == 1.0, 0.0, counts[1])).astype(jnp.int32)

    def back_copy(slot, to):
        return send(
            sent_context.at[slot, to], got_context.at[group * slots + slot],
            back_send.at[slot, to], back_recv.at[group * slots + slot], seq_device(to * members + member),
        )

    def stores(slot):
        return [
            pltpu.make_async_copy(queries.at[slot], far_queries.at[slot], store_sems.at[slot, 0]),
            pltpu.make_async_copy(pairs.at[slot], far_pairs.at[slot], store_sems.at[slot, 1]),
            pltpu.make_async_copy(outs.at[slot], far_outs.at[slot], store_sems.at[slot, 2]),
        ]

    def one_slot(slot, carry):
        for away in range(1, groups):
            origin = lax.rem(group + away, groups)
            arrived_pair(slot, origin).wait_recv()
            for beyond in range(1, members):
                pass_copy(slot, origin, beyond).start()
        for away in range(1, groups):
            origin = lax.rem(group + away, groups)
            arrived_query(slot, origin).wait_recv()
        for origin in range(groups):
            for beyond in range(1, members):
                passed(slot, origin, beyond).wait_recv()
        half_low = low_lanes((half, 2 * HEAD))
        for g in range(groups):
            packed = got_queries[slot, g].astype(F32)
            queries[slot, g, :half] = jnp.where(half_low, packed, 0.0).astype(BF16)
            queries[slot, g, half:] = jnp.where(half_low, swap_lanes(packed), 0.0).astype(BF16)
            query = queries[slot, g]
            scores = []
            for k in range(g + 1):
                tile = pairs[slot, k * members : (k + 1) * members].reshape(members * rows, 128)
                scores.append(hide(plan, back_product(tile, query), k, g, member, starts[g][:1]))
            top = functools.reduce(jnp.maximum, [jnp.max(s, axis=0, keepdims=True) for s in scores])
            total, out = 0.0, 0.0
            for k in range(g + 1):
                tile = pairs[slot, k * members : (k + 1) * members].reshape(members * rows, 128)
                chance = jnp.exp(scores[k] - top)
                total = total + jnp.sum(chance, axis=0, keepdims=True)
                out = out + outer_sum(tile, chance.astype(BF16))
            logs[slot, g] = jnp.broadcast_to(top + jnp.log(total), (8, rows))
            done = jnp.transpose(out / total)
            outs[slot, g] = done
            out_low = done.astype(BF16).astype(F32)
            packed_out = jnp.where(half_low, swap_lanes(out_low[:half]), out_low[half:]).astype(BF16)

            @pl.when(group != g)
            def _():
                sent_context[slot, g] = packed_out
                back_copy(slot, g).start()

            @pl.when(group == g)
            def _():
                got_context[group * slots + slot] = packed_out

        for copy in stores(slot):
            copy.start()
        return carry

    lax.fori_loop(0, slots, one_slot, 0)

    @pl.when(me < devices - 1)
    def _():
        edge_copy.wait_send()

    for slot in range(slots):
        for copy in stores(slot):
            copy.wait()
        for away in range(1, groups):
            origin = lax.rem(group + away, groups)
            pair_copy(slot, away).wait_send()
            query_copy(slot, away).wait_send()
            send(
                sent_context.at[slot, 0], got_context.at[origin * slots + slot],
                back_send.at[slot, 0], back_recv.at[origin * slots + slot], seq_device(me),
            ).wait_recv()
            back_copy(slot, origin).wait_send()
        for origin in range(groups):
            for beyond in range(1, members):
                pass_copy(slot, origin, beyond).wait_send()

    @pl.loop(0, stretches + 1)
    def _(s):
        memory_copy(s).wait()

    for two in range(HEADS // 2):
        first = got_context[2 * two].astype(F32)
        second = got_context[2 * two + 1].astype(F32)
        half_low = low_lanes((half, 2 * HEAD))
        columns = slice(two * 128, two * 128 + 128)
        context[:half, columns] = jnp.where(half_low, first, swap_lanes(second)).astype(BF16)
        context[half:, columns] = jnp.where(half_low, swap_lanes(first), second).astype(BF16)


def attend(plan, tokens, gain, shift, segments, weight, neighbours, memory_weight):
    devices, groups, members, slots, rows = plan.devices, plan.groups, plan.members, plan.slots, plan.rows
    half = rows // 2
    stretches = neighbours.shape[0] // SPAN
    dma = pltpu.SemaphoreType.DMA
    near = [
        ((rows, D), BF16),
        ((slots, groups, 8, rows), F32),
        ((groups, 8, rows), jnp.int32),
        ((rows, D), BF16),
        ((SPAN, D), BF16),
    ]
    far = [
        ((slots, groups, rows, 128), BF16),
        ((slots, devices, rows, 128), BF16),
        ((slots, groups, rows, 128), F32),
        ((stretches + 1, SPAN, 2 * D), BF16),
    ]
    vmem, hbm = pl.BlockSpec(memory_space=VM), pl.BlockSpec(memory_space=pl.ANY)
    return pl.pallas_call(
        partial(attend_kernel, plan),
        out_shape=[jax.ShapeDtypeStruct(*s) for s in near + far],
        in_specs=[vmem] * 4 + [hbm] * 3,
        out_specs=[vmem] * len(near) + [hbm] * len(far),
        scratch_shapes=[VM(*s) for s in far]
        + [
            VM(weight.shape, BF16),
            VM(neighbours.shape, BF16),
            VM(memory_weight.shape, BF16),
            VM((devices, 8, rows), F32),
            VM((rows, 3 * D), F32),
            VM((HEADS, rows, 128), BF16),
            VM((HEADS, half, 128), BF16),
            VM((slots, groups, half, 128), BF16),
            VM((slots, groups, half, 128), BF16),
            VM((HEADS, half, 128), BF16),
            dma((slots, groups)),
            dma((slots, groups)),
            dma((slots, groups)),
            dma((slots, groups)),
            dma((slots, groups, members)),
            dma((slots, devices)),
            dma((slots, groups)),
            dma((HEADS,)),
            dma((devices,)),
            dma((devices,)),
            dma,
            dma,
            dma((3,)),
            dma((stretches + 1,)),
            dma((slots, 3)),
        ],
        compiler_params=pltpu.CompilerParams(
            collective_id=0, has_side_effects=True, vmem_limit_bytes=60 << 20
        ),
        name="attend",
    )(tokens, gain, shift, segments, weight, neighbours, memory_weight)


class Grad:
    def __init__(self, matrix, first, count, at=0):
        self.matrix, self.first, self.count, self.at = matrix, first, count, at


class Product:
    def __init__(self, matrix, first, count, at=0):
        self.matrix, self.first, self.count, self.at = matrix, first, count, at


class Share:
    def __init__(self, rows, columns, order, pieces, vectors=None):
        self.rows, self.columns, self.order, self.pieces, self.vectors = rows, columns, order, pieces, vectors


def shares_of(batch, groups, ff):
    short, tall = D // (batch * groups), ff // (batch * groups * 2)
    half = D // 2
    return [
        Share(tall, half, "xyz", []),
        Share(tall, half, "yxz", []),
        Share(short, ff // 4, "xyz", [Product(0, 0, ff // 4)]),
        Share(short, ff // 4, "zyx", [Product(0, ff // 4, ff // 4)]),
        Share(short, 512, "xyz", [Grad(0, 0, 512)]),
        Share(short, 256 + half, "yxz", [Grad(0, 512, 256), Product(0, 0, half, 256)]),
        Share(short, half, "zxy", [Product(1, 0, half)]),
        Share(short, half, "zyx", [Product(2, 0, half)]),
        Share(short, 640, "xyz", [Product(3, 0, 640)]),
        Share(short, 640, "yxz", [Product(3, 640, 512)], vectors=512),
    ]


EARLY = 4


def part_shape(share, batch, axes):
    sizes = {"z": batch, "y": 2, "x": 2}
    return tuple(sizes[a] for a in axes) + (share.rows, share.columns)


def step_shapes(share, batch, axes, order):
    shapes = []
    for axis in order:
        axes = axes.replace(axis, "")
        lead = (batch - 1,) if axis == "z" else ()
        shapes.append(lead + part_shape(share, batch, axes))
    return shapes


def add(a, b):
    return (a.astype(F32) + b.astype(F32)).astype(BF16)


class Engine:
    def __init__(self, plan, batch, shares, sums, arrivals, gathered, send_sems, recv_sems, keep_sems):
        self.plan, self.batch, self.shares = plan, batch, shares
        self.sums, self.arrivals, self.gathered = sums, arrivals, gathered
        self.send_sems, self.recv_sems, self.keep_sems = send_sems, recv_sems, keep_sems
        me, group, member = plan.place()
        self.me, self.group, self.member = me, group, member
        self.z = lax.axis_index("batch")
        self.x, self.y = lax.rem(group, 2), lax.div(group, 2)
        self.partner = seq_device(group * plan.members + 1 - member)
        chip = lambda g: seq_device(g * plan.members + member)
        self.across = {"x": chip(self.y * 2 + 1 - self.x), "y": chip((1 - self.y) * 2 + self.x)}
        self.diagonal = chip((1 - self.y) * 2 + 1 - self.x)
        self.layers = [lax.rem(self.z + i, batch) for i in range(1, batch)]

    def peers(self):
        return [self.partner, self.across["x"], self.across["y"], self.diagonal] + [
            (self.me, layer) for layer in self.layers
        ]

    def steps(self, s, fill, axes, order, stop=None):
        total, share = self.sums[s], self.shares[s]
        own = {"x": self.x, "y": self.y, "z": self.z}
        count = 0

        def sems():
            nonlocal count
            count += 1
            return self.send_sems.at[s, count - 1], self.recv_sems.at[s, count - 1]

        fill()
        done = {}
        for number, axis in enumerate(order):
            where = lambda spots: tuple(spots.get(a, slice(None)) for a in axes)
            arrived = self.arrivals[s][number]
            copies = []
            if axis == "z":
                for i, layer in enumerate(self.layers):
                    copies.append(
                        send(total.at[where({**done, "z": layer})], arrived.at[i], *sems(), (self.me, layer))
                    )
            else:
                copies.append(
                    send(total.at[where({**done, axis: 1 - own[axis]})], arrived, *sems(), self.across[axis])
                )
            for copy in copies:
                copy.start()
            yield
            for copy in copies:
                copy.wait()
            done[axis] = own[axis]
            spot = where(done)
            value = total[spot].astype(F32)
            if axis == "z":
                for i in range(self.batch - 1):
                    value = value + arrived[i].astype(F32)
            else:
                value = value + arrived[...].astype(F32)
            if stop is None:
                total[spot] = value.astype(BF16)
            else:
                stop[...] = value.astype(BF16)
        if stop is not None:
            return
        out = self.gathered[s]
        block = total.at[where(done)]
        first, second = share.order.replace("z", "")[::-1]
        home = out.at[self.member, self.y, self.x]
        keep = pltpu.make_async_copy(block, home, self.keep_sems.at[s])
        keep.start()
        copy = send(block, home, *sems(), self.across[first])
        copy.start()
        yield
        copy.wait()
        came = (self.member, 1 - self.y, self.x) if first == "y" else (self.member, self.y, 1 - self.x)
        copies = [send(block, home, *sems(), self.across[second])]
        copies.append(send(out.at[came], out.at[came], *sems(), self.across[second]))
        for copy in copies:
            copy.start()
        keep.wait()
        yield
        for copy in copies:
            copy.wait()
        copy = send(out.at[self.member], out.at[self.member], *sems(), self.partner)
        copy.start()
        yield
        copy.wait()


def spread_to(target, rows, values, at):
    layers, groups = target.shape[0], target.shape[1] * target.shape[2]
    for layer in range(layers):
        for g in range(groups):
            start = (layer * groups + g) * rows
            target[layer, g // 2, g % 2, :, pl.ds(at, values.shape[1])] = values[start : start + rows].astype(BF16)


def tail_kernel(plan, batch, shares, arrival_counts, names, *refs):
    r = dict(zip(names, refs))
    refs = refs[len(names) :]
    takes = iter(refs)
    neighbour_grad = next(takes)
    gathered = [next(takes) for _ in shares]
    two_left = [next(takes) for _ in range(4)]
    two_right = [next(takes) for _ in range(4)]
    sums = [next(takes) for _ in shares]
    arrivals = [[next(takes) for _ in range(n)] for n in arrival_counts]
    grad_pieces = [piece for share in shares for piece in share.pieces if isinstance(piece, Grad)]
    other_grads = [next(takes) for _ in grad_pieces]
    (
        queries, pairs, outs, pack_grads, got_grads, grads, deltas, pair_sum, query_sum,
        give, took, sent_pair, got_pair, sent_query, got_query, result, vector_rows, other_rows,
        near, slopes, memory_weight, give_grads, stage, edge_sent, edge_got,
        load_sems, out_send, out_recv, give_send, give_recv, pair_send, pair_recv, query_send, query_recv,
        own_sems, swap_send, swap_recv, piece_send, piece_recv, state_sems, near_sems, stage_sems, edge_send, edge_recv, send_sems, recv_sems, keep_sems,
    ) = takes
    me, group, member = plan.place()
    devices, groups, members, slots, rows = plan.devices, plan.groups, plan.members, plan.slots, plan.rows
    half = rows // 2
    half_low = low_lanes((half, 2 * HEAD))
    low = low_lanes((rows, 2 * HEAD))
    engine = Engine(plan, batch, shares, sums, arrivals, gathered, send_sems, recv_sems, keep_sems)
    partner = engine.partner
    before = jnp.maximum(me - 1, 0)
    greet(
        [seq_device(lax.rem(me + i, devices)) for i in range(1, devices)]
        + [(me, layer) for layer in engine.layers]
    )

    def load(slot):
        spot = slot % 2
        return [
            pltpu.make_async_copy(r["queries"].at[slot], queries.at[spot], load_sems.at[spot, 0]),
            pltpu.make_async_copy(r["pairs"].at[slot], pairs.at[spot], load_sems.at[spot, 1]),
            pltpu.make_async_copy(r["outs"].at[slot], outs.at[spot], load_sems.at[spot, 2]),
        ]

    for copy in load(0):
        copy.start()
    for head in range(HEADS):
        block = (head // 2) * 128
        pack_grads[head] = pack_rows(r["grad_out"][:, block : block + 128].astype(F32), head).astype(BF16)

    def out_copy(slot, away):
        to = lax.rem(group + away, groups)
        return send(
            pack_grads.at[to * slots + slot], got_grads.at[slot, group],
            out_send.at[slot, away - 1], out_recv.at[slot, group], seq_device(to * members + member),
        )

    for slot in range(slots):
        for away in range(1, groups):
            out_copy(slot, away).start()
        got_grads[slot, group] = pack_grads[group * slots + slot]

    state_loads = [
        pltpu.make_async_copy(r["state%d" % s], sums[s], state_sems.at[s]) for s in range(EARLY)
    ]
    stretches = r["neighbours"].shape[0] // SPAN
    near_loads = [
        pltpu.make_async_copy(r["edge"], near.at[pl.ds(0, SPAN)], near_sems.at[0]),
        pltpu.make_async_copy(r["neighbours"], near.at[pl.ds(SPAN, stretches * SPAN)], near_sems.at[1]),
        pltpu.make_async_copy(r["memory_grad"], slopes, near_sems.at[2]),
        pltpu.make_async_copy(r["memory_weight"], memory_weight, near_sems.at[3]),
    ]
    for copy in near_loads + state_loads:
        copy.start()

    lefts = [r["left%d" % m] for m in range(4)]
    rights = [r["right%d" % m] for m in range(3)] + [result]
    here, there = pl.ds(0, rows), pl.ds(rows, rows)

    def left_swaps(m):
        return [
            pltpu.make_async_copy(lefts[m], two_left[m].at[here], own_sems.at[m, 0]),
            send(lefts[m], two_left[m].at[there], swap_send.at[m, 0], swap_recv.at[m, 0], partner),
        ]

    def right_swaps(m):
        width = rights[m].shape[1] // 2
        mine = pl.ds(pl.multiple_of(member * width, 128), width)
        theirs = pl.ds(pl.multiple_of((1 - member) * width, 128), width)
        return [
            pltpu.make_async_copy(rights[m].at[:, mine], two_right[m].at[here], own_sems.at[m, 1]),
            send(rights[m].at[:, theirs], two_right[m].at[there], swap_send.at[m, 1], swap_recv.at[m, 1], partner),
        ]

    swaps = {}
    for m in range(3):
        swaps[m] = left_swaps(m) + right_swaps(m)
        for copy in swaps[m]:
            copy.start()
    last_left = left_swaps(3)
    for copy in last_left:
        copy.start()

    pieces = {}
    for s, share in enumerate(shares):
        for piece in share.pieces:
            if isinstance(piece, Grad):
                n = len(pieces)
                pieces[piece] = (n, s, send(
                    give_grads.at[:, :, :, :, pl.ds(piece.first, piece.count)], other_grads[n],
                    piece_send.at[n], piece_recv.at[n], partner,
                ))

    def memory_grads():
        for copy in near_loads:
            copy.wait()
        width = slopes.shape[1] // 2
        for piece, (n, s, copy) in pieces.items():
            for first in range(piece.first, piece.first + piece.count, 256):
                columns = pl.ds(pl.multiple_of((1 - member) * width + first, 256), 256)
                spread_to(give_grads, shares[s].rows, outer_sum(near[...], slopes[:, columns]), first)
            copy.start()
        for piece, (n, s, copy) in pieces.items():
            for first in range(piece.first, piece.first + piece.count, 256):
                columns = pl.ds(pl.multiple_of(member * width + first, 256), 256)
                spread(s, outer_sum(near[...], slopes[:, columns]), piece.at + first - piece.first)

    def edge_copy():
        return send(edge_sent, edge_got, edge_send, edge_recv, seq_device(before))

    def stage_copy(s):
        return pltpu.make_async_copy(
            stage.at[s % 2], neighbour_grad.at[pl.ds(s * SPAN, SPAN)], stage_sems.at[s % 2]
        )

    def neighbour_grads(numbers):
        for s in numbers:
            if s >= 2:
                stage_copy(s - 2).wait()
            part = back_product(slopes[(s + 1) * SPAN : (s + 2) * SPAN, :], memory_weight[...])
            stage[s % 2] = part.astype(BF16)
            if s == stretches - 1:

                @pl.when(me < devices - 1)
                def _():
                    edge_copy().wait_recv()
                    stage[s % 2] = (part + edge_got[...].astype(F32)).astype(BF16)

            stage_copy(s).start()

    waited = set()

    def spread(s, values, at):
        spread_to(sums[s], shares[s].rows, values, at)

    def fill(s):
        for piece in shares[s].pieces:
            if isinstance(piece, Grad):
                n, _, copy = pieces[piece]
                copy.wait()
                for layer in range(batch):
                    columns = pl.ds(piece.at, piece.count)
                    sums[s][layer, :, :, :, columns] = add(sums[s][layer, :, :, :, columns], other_grads[n][layer])
            else:
                m = piece.matrix
                if m not in waited:
                    waited.add(m)
                    for copy in swaps[m]:
                        copy.wait()
                tile = 384 if piece.count % 384 == 0 else 512 if piece.count % 512 == 0 else 128
                for t in range(piece.count // tile):
                    first = piece.first + t * tile
                    spread(s, outer_sum(two_left[m][...], two_right[m][:, first : first + tile]), piece.at + t * tile)
        if shares[s].vectors is not None:
            vector_copy.wait()
            mine = vector_rows[member] + other_rows[...]
            wide = jnp.concatenate([mine, jnp.zeros((120, D), F32)], axis=0)
            spread(s, jnp.transpose(wide), shares[s].vectors)

    def ready(s):
        state_loads[s].wait()

    running = []
    for s, share in enumerate(shares):
        if s < EARLY:
            axes = "zyx".replace(share.order[0], "")
            running.append(engine.steps(s, partial(ready, s), axes, share.order[1:]))
        else:
            running.append(engine.steps(s, partial(fill, s), "zyx", share.order))

    def advance(*numbers):
        for n in numbers:
            next(running[n], None)

    advance(0, 1, 2, 3)
    memory_grads()
    advance(4, 5)
    edge_sent[...] = back_product(slopes[0:SPAN, :], memory_weight[...]).astype(BF16)

    @pl.when(me > 0)
    def _():
        edge_copy().start()

    advance(6, 7)

    def give_copy(slot, away):
        to = lax.rem(member + away, members)
        return send(
            give.at[away - 1], took.at[slot, away - 1],
            give_send.at[slot, away - 1], give_recv.at[slot, away - 1], seq_device(group * members + to),
        )

    def pair_copy(slot, to):
        return send(
            sent_pair.at[to], got_pair.at[group * slots + slot],
            pair_send.at[slot, to], pair_recv.at[group * slots + slot], seq_device(to * members + member),
        )

    def query_copy(slot, to):
        return send(
            sent_query.at[slot, to], got_query.at[group * slots + slot],
            query_send.at[slot, to], query_recv.at[group * slots + slot], seq_device(to * members + member),
        )

    between = [(0, 1, 2, 3), (0, 1, 2, 3, 4, 5), (0, 1, 2, 3, 6, 7)]
    for slot in range(slots):
        spot = slot % 2
        for copy in load(slot):
            copy.wait()
        if slot + 1 < slots:
            for copy in load(slot + 1):
                copy.start()
        for away in range(1, groups):
            origin = lax.rem(group + away, groups)
            send(
                pack_grads.at[0], got_grads.at[slot, origin],
                out_send.at[slot, 0], out_recv.at[slot, origin], partner,
            ).wait_recv()
        for g in range(groups):
            packed = got_grads[slot, g].astype(F32)
            top = jnp.where(half_low, 0.0, swap_lanes(packed))
            bottom = jnp.where(half_low, 0.0, packed)
            grads[g, :half] = top.astype(BF16)
            grads[g, half:] = bottom.astype(BF16)
            product = jnp.concatenate([top, bottom], axis=0) * outs[spot, g]
            deltas[g] = jnp.broadcast_to(jnp.sum(jnp.transpose(product), axis=0, keepdims=True), (8, rows))
        for k in range(groups):
            total = 0.0
            tile = pairs[spot, k * members : (k + 1) * members].reshape(members * rows, 128)
            for g in range(k, groups):
                query, grad = queries[spot, g], grads[g]
                scores = hide(plan, back_product(tile, query), k, g, member, r["starts"][g][:1])
                chance = jnp.exp(scores - r["logs"][slot, g][:1])
                chance_grad = back_product(tile, grad)
                score_grad = (chance * (chance_grad - deltas[g][:1])).astype(BF16)
                total = total + matmul(score_grad, query) + matmul(chance.astype(BF16), grad)
                part = outer_sum(tile, score_grad)
                query_sum[g] = part if k == 0 else query_sum[g] + part
            pair_sum[k * members : (k + 1) * members] = total.reshape(members, rows, 128)
        for away in range(1, members):
            to = lax.rem(member + away, members)
            if slot > 0:
                give_copy(slot - 1, away).wait_send()
            for g in range(groups):
                give[away - 1, g] = pair_sum[g * members + to].astype(BF16)
            give_copy(slot, away).start()
        for g in range(groups):
            total = jnp.transpose(query_sum[g]) * (HEAD ** -0.5)
            packed = jnp.where(half_low, total[:half], swap_lanes(total[half:])).astype(BF16)

            @pl.when(group != g)
            def _():
                sent_query[slot, g] = packed
                query_copy(slot, g).start()

            @pl.when(group == g)
            def _():
                got_query[group * slots + slot] = packed

        for away in range(1, members):
            give_copy(slot, away).wait_recv()
        for g in range(groups):
            total = pair_sum[g * members + member]
            for away in range(1, members):
                total = total + took[slot, away - 1, g].astype(F32)
            total = total.astype(BF16)

            @pl.when(group != g)
            def _():
                if slot > 0:
                    pair_copy(slot - 1, g).wait_send()
                sent_pair[g] = total
                pair_copy(slot, g).start()

            @pl.when(group == g)
            def _():
                got_pair[group * slots + slot] = total

        advance(*between[slot])

    neighbour_grads(range(stretches))
    wide, narrow = slopes.at[pl.ds(0, D)], slopes.at[pl.ds(D, D), pl.ds(0, D)]
    weight_loads = [
        pltpu.make_async_copy(r["weight"].at[:, pl.ds(0, 2 * D)], wide, load_sems.at[0, 3]),
        pltpu.make_async_copy(r["weight"].at[:, pl.ds(2 * D, D)], narrow, load_sems.at[1, 3]),
    ]
    for copy in weight_loads:
        copy.start()
    for slot in range(slots):
        for away in range(1, groups):
            origin = lax.rem(group + away, groups)
            head = origin * slots + slot
            send(
                sent_query.at[slot, 0], got_query.at[head],
                query_send.at[slot, 0], query_recv.at[head], partner,
            ).wait_recv()
            send(
                sent_pair.at[0], got_pair.at[head], pair_send.at[slot, 0], pair_recv.at[head], partner,
            ).wait_recv()
    for two in range(HEADS // 2):
        columns = slice(two * 128, two * 128 + 128)
        first = got_query[2 * two].astype(F32)
        second = got_query[2 * two + 1].astype(F32)
        result[:half, columns] = jnp.where(half_low, first, swap_lanes(second)).astype(BF16)
        result[half:, columns] = jnp.where(half_low, swap_lanes(first), second).astype(BF16)
        first = got_pair[2 * two].astype(F32)
        second = got_pair[2 * two + 1].astype(F32)
        result[:, slice(D + two * 128, D + two * 128 + 128)] = jnp.where(low, first, swap_lanes(second)).astype(BF16)
        result[:, slice(2 * D + two * 128, 2 * D + two * 128 + 128)] = jnp.where(
            low, swap_lanes(first), second
        ).astype(BF16)
    swaps[3] = last_left + right_swaps(3)
    for copy in swaps[3][2:]:
        copy.start()
    for copy in weight_loads:
        copy.wait()
    normed_grad = back_product(result[:, : 2 * D], wide[...]) + back_product(result[:, 2 * D :], narrow[...])
    values = r["tokens"][...].astype(F32)
    centred = values - jnp.mean(values, axis=1, keepdims=True)
    inverse = lax.rsqrt(jnp.mean(centred * centred, axis=1, keepdims=True) + EPSILON)
    unit = centred * inverse
    vector_rows[0] = jnp.concatenate(
        [jnp.sum(normed_grad * unit, axis=0, keepdims=True), r["vectors"][0:2], jnp.zeros((5, D), F32)], axis=0
    )
    vector_rows[1] = jnp.concatenate(
        [jnp.sum(normed_grad, axis=0, keepdims=True), r["vectors"][2:4], jnp.zeros((5, D), F32)], axis=0
    )
    vector_copy = send(
        vector_rows.at[1 - member], other_rows, swap_send.at[4, 0], swap_recv.at[4, 0], partner
    )
    vector_copy.start()
    advance(8)
    scaled = normed_grad * as_row(r["gain"])
    input_grad = r["stream_grad"][...] + inverse * (
        scaled
        - jnp.mean(scaled, axis=1, keepdims=True)
        - unit * jnp.mean(scaled * unit, axis=1, keepdims=True)
    )
    r["input_grad"][...] = input_grad.astype(BF16)
    advance(9)
    for _ in range(7):
        advance(6, 7, 4, 5, 2, 3, 0, 1, 8, 9)

    for s in range(max(stretches - 2, 0), stretches):
        stage_copy(s).wait()

    @pl.when(me > 0)
    def _():
        edge_copy().wait_send()

    for slot in range(slots):
        for away in range(1, members):
            if slot == slots - 1:
                give_copy(slot, away).wait_send()
        for away in range(1, groups):
            origin = lax.rem(group + away, groups)
            out_copy(slot, away).wait_send()
            if slot == slots - 1:
                pair_copy(slot, origin).wait_send()
            query_copy(slot, origin).wait_send()


def tail(plan, batch, grad_out, queries, pairs, outs, logs, starts, lefts, rights, states,
    neighbours, edge, memory_grad, memory_weight, weight, tokens, gain, stream_grad, vectors, ff,
):
    devices, groups, members, slots, rows = plan.devices, plan.groups, plan.members, plan.slots, plan.rows
    half = rows // 2
    shares = shares_of(batch, groups, ff)
    dma = pltpu.SemaphoreType.DMA
    inputs = {"grad_out": grad_out, "logs": logs, "starts": starts, "tokens": tokens, "gain": gain}
    inputs.update(stream_grad=stream_grad, vectors=vectors)
    small = len(inputs)
    inputs.update(queries=queries, pairs=pairs, outs=outs, weight=weight)
    inputs.update({"left%d" % m: left for m, left in enumerate(lefts)})
    inputs.update({"right%d" % m: right for m, right in enumerate(rights)})
    inputs.update({"state%d" % m: state for m, state in enumerate(states)})
    inputs.update(neighbours=neighbours, edge=edge, memory_grad=memory_grad, memory_weight=memory_weight)
    widths = [right.shape[1] // 2 for right in rights] + [3 * D // 2]
    axes = ["zyx".replace(s.order[0], "") if n < EARLY else "zyx" for n, s in enumerate(shares)]
    orders = [s.order[1:] if n < EARLY else s.order for n, s in enumerate(shares)]
    steps = [step_shapes(share, batch, axes[n], orders[n]) for n, share in enumerate(shares)]
    scratch = [VM((2 * rows, left.shape[1]), BF16) for left in lefts]
    scratch += [VM((2 * rows, width), BF16) for width in widths]
    scratch += [VM(part_shape(share, batch, axes[n]), BF16) for n, share in enumerate(shares)]
    scratch += [VM(shape, BF16) for shapes in steps for shape in shapes]
    scratch += [
        VM((batch, 2, 2, share.rows, piece.count), BF16)
        for share in shares[EARLY:]
        for piece in share.pieces
        if isinstance(piece, Grad)
    ]
    span_rows = memory_grad.shape[0]
    scratch += [
        VM((2, groups, rows, 128), BF16),
        VM((2, devices, rows, 128), BF16),
        VM((2, groups, rows, 128), F32),
        VM((HEADS, half, 128), BF16),
        VM((slots, groups, half, 128), BF16),
        VM((groups, rows, 128), BF16),
        VM((groups, 8, rows), F32),
        VM((devices, rows, 128), F32),
        VM((groups, 128, rows), F32),
        VM((members - 1, groups, rows, 128), BF16),
        VM((slots, members - 1, groups, rows, 128), BF16),
        VM((groups, rows, 128), BF16),
        VM((HEADS, rows, 128), BF16),
        VM((slots, groups, half, 128), BF16),
        VM((HEADS, half, 128), BF16),
        VM((rows, 3 * D), BF16),
        VM((2, 8, D), F32),
        VM((8, D), F32),
        VM((span_rows, D), BF16),
        VM((span_rows, 2 * D), BF16),
        VM((D, 2 * D), BF16),
        VM((batch, 2, 2, shares[EARLY].rows, D), BF16),
        VM((2, SPAN, D), BF16),
        VM((SPAN, D), BF16),
        VM((SPAN, D), BF16),
        dma((2, 4)),
        dma((slots, groups)),
        dma((slots, groups)),
        dma((slots, members - 1)),
        dma((slots, members - 1)),
        dma((slots, groups)),
        dma((HEADS,)),
        dma((slots, groups)),
        dma((HEADS,)),
        dma((4, 2)),
        dma((5, 2)),
        dma((5, 2)),
        dma((2,)),
        dma((2,)),
        dma((EARLY,)),
        dma((4,)),
        dma((2,)),
        dma,
        dma,
        dma((len(shares), 6 + batch)),
        dma((len(shares), 6 + batch)),
        dma((len(shares),)),
    ]
    names = list(inputs) + ["input_grad"]
    out = pl.pallas_call(
        partial(tail_kernel, plan, batch, shares, [len(s) for s in steps], names),
        out_shape=[jax.ShapeDtypeStruct((rows, D), BF16), jax.ShapeDtypeStruct(neighbours.shape, BF16)]
        + [jax.ShapeDtypeStruct((2, 2, 2, s.rows, s.columns), BF16) for s in shares],
        in_specs=[pl.BlockSpec(memory_space=VM)] * small + [pl.BlockSpec(memory_space=pl.ANY)] * (len(inputs) - small),
        out_specs=[pl.BlockSpec(memory_space=VM)] + [pl.BlockSpec(memory_space=pl.ANY)] * (1 + len(shares)),
        scratch_shapes=scratch,
        compiler_params=pltpu.CompilerParams(
            collective_id=1, has_side_effects=True, vmem_limit_bytes=62 << 20
        ),
        name="tail",
    )(*inputs.values())
    return out[0], out[1], out[2:]


def widen_kernel(batch, *refs):
    shares, (low_result, low_input, low_neighbour) = refs[:10], refs[10:13]
    down, up, cross_out, memory, query, self_out, self_weight, result, input_grad, neighbour_grad = refs[13:23]
    vectors, kept = refs[23:29], refs[29]
    step = pl.program_id(0)

    def put(out, s, at, first, count):
        for core in range(2):
            width = out.shape[1] // 2
            block = shares[s][core, 0, 0, :, first : first + count]
            out[:, core * width + at : core * width + at + count] = block.astype(F32)

    for part in range(2):
        for core in range(2):
            rows = shares[part].shape[3]
            out_rows = slice(part * rows, part * rows + rows)
            down[out_rows, core * (D // 2) : (core + 1) * (D // 2)] = shares[part][core, 0, 0].astype(F32)
    quarter = up.shape[1] // 4
    put(up, 2, 0, 0, quarter)
    put(up, 3, quarter, 0, quarter)
    put(memory, 4, 0, 0, 512)
    put(memory, 5, 512, 0, 256)
    put(cross_out, 5, 0, 256, D // 2)
    put(query, 6, 0, 0, D // 2)
    put(self_out, 7, 0, 0, D // 2)
    put(self_weight, 8, 0, 0, 640)
    put(self_weight, 9, 640, 0, 512)
    result[...] = low_result[...]
    input_grad[...] = low_input[...].astype(F32)
    neighbour_grad[...] = low_neighbour[...].astype(F32)
    rows = shares[9].shape[3]
    for core in range(2):
        kept[core, pl.ds(pl.multiple_of(step * rows, 16), rows)] = shares[9][core, 0, 0, :, 512:].astype(F32)

    @pl.when(step == 3)
    def _():
        for core in range(2):
            turned = jnp.transpose(kept[core])
            for n in range(3):
                vectors[core * 3 + n][...] = turned[n]


def widen(plan, batch, ff, shares, result, input_grad, neighbour_grad):
    rows = plan.rows
    ins = [pl.BlockSpec((2, 1, 1) + s.shape[3:], lambda i: (0, i // 2, i % 2, 0, 0)) for s in shares]
    passed = [result, input_grad, neighbour_grad]
    ins += [pl.BlockSpec((a.shape[0] // 4, D), lambda i: (i, 0)) for a in passed]
    layout = [(ff, D), (D, ff), (D, D), (D, 2 * D), (D, D), (D, D), (D, 3 * D)]
    layout = [(r // batch, c) for r, c in layout] + [a.shape for a in passed]
    kinds = [F32] * 7 + [BF16, F32, F32]
    outs = [pl.BlockSpec((r // 4, c), lambda i: (i, 0)) for r, c in layout]
    outs += [pl.BlockSpec((D // batch,), lambda i: (0,))] * 6
    return pl.pallas_call(
        partial(widen_kernel, batch),
        grid=(4,),
        in_specs=ins,
        out_specs=outs,
        out_shape=[jax.ShapeDtypeStruct(shape, kind) for shape, kind in zip(layout, kinds)]
        + [jax.ShapeDtypeStruct((D // batch,), F32)] * 6,
        scratch_shapes=[VM((2, D // batch, 128), F32)],
        compiler_params=pltpu.CompilerParams(vmem_limit_bytes=60 << 20),
        name="widen",
    )(*shares, *passed)


FOLD = 256 // HEAD


def stack_heads(values):
    lane = lax.broadcasted_iota(jnp.int32, values.shape, 1) // HEAD
    return jnp.concatenate([jnp.where(lane == h, values, jnp.zeros_like(values)) for h in range(FOLD)], axis=0)


def unstack_heads(stacked):
    count = stacked.shape[0] // FOLD
    lane = lax.broadcasted_iota(jnp.int32, (count, stacked.shape[1]), 1) // HEAD
    total = jnp.where(lane == 0, stacked[:count], 0.0)
    for h in range(1, FOLD):
        total = total + jnp.where(lane == h, stacked[h * count : (h + 1) * count], 0.0)
    return total


def cross_chances(queries, keys):
    scores = back_product(queries, keys)
    chance = jnp.exp(scores - jnp.max(scores, axis=1, keepdims=True))
    return chance / jnp.sum(chance, axis=1, keepdims=True)


def norm_parts(values):
    centred = values - jnp.mean(values, axis=1, keepdims=True)
    inverse = lax.rsqrt(jnp.mean(centred * centred, axis=1, keepdims=True) + EPSILON)
    return centred * inverse, inverse


def norm_back(values, gain, grad):
    unit, inverse = norm_parts(values)
    scaled = grad * gain
    inner = inverse * (
        scaled - jnp.mean(scaled, axis=1, keepdims=True) - unit * jnp.mean(scaled * unit, axis=1, keepdims=True)
    )
    return jnp.sum(grad * unit, axis=0, keepdims=True), jnp.sum(grad, axis=0, keepdims=True), inner


def middle_kernel(plan, batch, shares, arrival_counts, names, *refs):
    r = dict(zip(names, refs))
    takes = iter(refs[len(names) :])
    sums = [next(takes) for _ in range(EARLY)]
    arrivals = [[next(takes) for _ in range(n)] for n in arrival_counts]
    (
        up, down, active, two_normed, give_upper, two_upper, two_grad, slopes,
        stream_one, stream_two, normed_grad, summed, moved_queries, moved_grads, moved,
        load_sems, own_sems, tile_send, tile_recv, swap_send, swap_recv, group_sems, send_sems, recv_sems,
    ) = takes
    me, group, member = plan.place()
    rows, groups = plan.rows, plan.groups
    states = [r["state%d" % s] for s in range(EARLY)]
    engine = Engine(plan, batch, shares, sums, arrivals, None, send_sems, recv_sems, None)
    partner = engine.partner
    greet(engine.peers())
    here, there = pl.ds(0, rows), pl.ds(rows, rows)
    ff = up.shape[1]
    loads = [
        pltpu.make_async_copy(r["memory"], slopes, load_sems.at[2]),
        pltpu.make_async_copy(r["up_weight"], up, load_sems.at[0]),
        pltpu.make_async_copy(r["down_weight"], down, load_sems.at[1]),
    ]
    for copy in loads:
        copy.start()
    half = D // 2
    mine = pl.ds(pl.multiple_of(member * half, 128), half)
    theirs = pl.ds(pl.multiple_of((1 - member) * half, 128), half)
    grad_swap = [
        pltpu.make_async_copy(r["cotangent"].at[:, mine], two_grad.at[here], own_sems.at[0]),
        send(r["cotangent"].at[:, theirs], two_grad.at[there], swap_send.at[0], swap_recv.at[0], partner),
    ]
    for copy in grad_swap:
        copy.start()
    at = lax.broadcasted_iota(jnp.int32, (rows, 1), 0)
    keep = ((me > 0) | (at >= STRETCH - 1)).astype(F32)
    stretches = slopes.shape[0]

    def move(values):
        wide = jnp.concatenate([values, jnp.zeros((STRETCH, D), F32)], axis=0)
        return pltpu.roll(wide, 1, 0).astype(BF16).reshape(stretches, STRETCH, D)

    def move_back():
        whole = moved[...].reshape(stretches * STRETCH, D)
        return pltpu.roll(whole, stretches * STRETCH - 1, 0)[:rows]

    stream_one[...] = r["tokens"][...].astype(F32) + matmul(r["context"][...], r["self_output"][...])
    normed_two = (norm_parts(stream_one[...])[0] * as_row(r["second_gain"]) + as_row(r["second_shift"])).astype(BF16)
    r["normed_two"][...] = normed_two
    cross_queries = matmul(normed_two, r["query_weight"][...]).astype(BF16).astype(F32) * (HEAD ** -0.5)
    moved_queries[...] = move(cross_queries)
    loads[0].wait()

    @pl.loop(0, stretches)
    def _(i):
        for c in range(D // 256):
            columns = slice(c * 256, c * 256 + 256)
            values = slice(D + c * 256, D + c * 256 + 256)
            chances = cross_chances(stack_heads(moved_queries[i, :, columns]), slopes[i, :, columns])
            moved[i, :, columns] = unstack_heads(matmul(chances.astype(BF16), slopes[i, :, values]))

    cross_low = (move_back() * keep).astype(BF16)
    r["cross_low"][...] = cross_low
    stream_two[...] = stream_one[...] + matmul(cross_low, r["cross_output"][...])
    two_normed[here] = (norm_parts(stream_two[...])[0] * as_row(r["third_gain"]) + as_row(r["third_shift"])).astype(BF16)
    normed_swap = send(two_normed.at[here], two_normed.at[there], swap_send.at[1], swap_recv.at[1], partner)
    normed_swap.start()
    normed_grad[...] = jnp.zeros_like(normed_grad)
    summed[...] = jnp.zeros_like(summed)
    for copy in loads[1:]:
        copy.wait()
    tile = 512
    tiles = ff // tile

    def tile_copy(t):
        columns = pl.ds(pl.multiple_of(t * tile, tile), tile)
        return send(
            active.at[here, columns], active.at[there, columns], tile_send.at[t], tile_recv.at[t], partner
        )

    @pl.loop(0, tiles)
    def _(t):
        columns = pl.ds(pl.multiple_of(t * tile, tile), tile)
        upper = matmul(two_normed[here], up[:, columns])
        density = jnp.exp(upper * upper * -0.5) * (2.0 * math.pi) ** -0.5
        below = 0.5 + 0.5 * lax.erf(upper * 0.5 ** 0.5)
        active_low = (upper * below).astype(BF16)
        active[here, columns] = active_low
        tile_copy(t).start()
        grad = back_product(r["cotangent"][...], down[columns])
        upper_low = (grad * (below + upper * density)).astype(BF16)
        spot = pl.ds(pl.multiple_of(lax.rem(t, tiles // 2) * tile, tile), tile)

        @pl.when(lax.div(t, tiles // 2) == member)
        def _():
            two_upper[here, spot] = upper_low

        @pl.when(lax.div(t, tiles // 2) != member)
        def _():
            give_upper[:, spot] = upper_low

        summed[...] += matmul(active_low, down[columns])
        normed_grad[...] += back_product(upper_low, up[:, columns])

    upper_swap = send(give_upper, two_upper.at[there], swap_send.at[2], swap_recv.at[2], partner)
    upper_swap.start()
    r["result"][...] = (stream_two[...] + summed[...]).astype(BF16)

    def fill_down(s):
        if s > 0:
            return
        for copy in grad_swap:
            copy.wait()

        @pl.loop(0, tiles)
        def _(t):
            tile_copy(t).wait()

        deep = ff // batch
        tall = shares[0].rows
        for layer in range(batch):
            values = outer_sum(active[:, layer * deep : (layer + 1) * deep], two_grad[...]).astype(BF16)
            for g in range(groups):
                for part in range(2):
                    start = (g * 2 + part) * tall
                    sums[part][layer, g // 2, g % 2] = values[start : start + tall]

    def fill_up(s):
        if s == 2:
            normed_swap.wait()
            upper_swap.wait()
        piece = shares[s].pieces[0]
        for first in range(0, piece.count, 384):
            tile_values = outer_sum(two_normed[...], two_upper[:, piece.first + first : piece.first + first + 384])
            spread_to(sums[s], shares[s].rows, tile_values, first)

    fills = [fill_down, fill_down, fill_up, fill_up]
    running = [
        engine.steps(s, partial(fills[s], s), "zyx", shares[s].order[:1], states[s]) for s in range(EARLY)
    ]
    for run in running:
        next(run, None)

    gain_grad, shift_grad, inner = norm_back(stream_two[...], as_row(r["third_gain"]), normed_grad[...])
    r["vectors"][1:2] = gain_grad
    r["vectors"][3:4] = shift_grad
    stream_two_grad = r["cotangent"][...].astype(F32) + inner
    normed_grad[...] = stream_two_grad
    branch_low = stream_two_grad.astype(BF16)
    r["branch"][...] = branch_low
    moved_grads[...] = move(back_product(branch_low, r["cross_output"][...]) * keep)

    def group_copy(i):
        return pltpu.make_async_copy(slopes.at[i], r["memory_grad"].at[i], group_sems.at[i])

    @pl.loop(0, stretches)
    def _(i):
        for c in range(D // 256):
            columns = slice(c * 256, c * 256 + 256)
            values = slice(D + c * 256, D + c * 256 + 256)
            stacked = stack_heads(moved_queries[i, :, columns])
            stacked_grad = stack_heads(moved_grads[i, :, columns])
            keys = slopes[i, :, columns]
            chances = cross_chances(stacked, keys)
            chance_grad = back_product(stacked_grad, slopes[i, :, values])
            total = jnp.sum(chances * chance_grad, axis=1, keepdims=True)
            score_grad = (chances * (chance_grad - total)).astype(BF16)
            moved[i, :, columns] = unstack_heads(matmul(score_grad, keys)) * (HEAD ** -0.5)
            slopes[i, :, columns] = outer_sum(score_grad, stacked).astype(BF16)
            slopes[i, :, values] = outer_sum(chances.astype(BF16), stacked_grad).astype(BF16)
        group_copy(i).start()

    query_grad = move_back().astype(BF16)
    r["query_grad"][...] = query_grad
    gain_grad, shift_grad, inner = norm_back(
        stream_one[...], as_row(r["second_gain"]), back_product(query_grad, r["query_weight"][...])
    )
    r["vectors"][0:1] = gain_grad
    r["vectors"][2:3] = shift_grad
    r["vectors"][4:8] = jnp.zeros((4, D), F32)
    stream_one_grad = normed_grad[...] + inner
    r["stream_grad"][...] = stream_one_grad
    self_low = stream_one_grad.astype(BF16)
    r["self_low"][...] = self_low
    r["grad_out"][...] = back_product(self_low, r["self_output"][...]).astype(BF16)
    for run in running:
        next(run, None)

    @pl.loop(0, stretches)
    def _(i):
        group_copy(i).wait()


def middle(plan, batch, tokens, context, self_output, second_gain, second_shift, third_gain, third_shift, query_weight, memory, cross_output, up_weight, down_weight, cotangent):
    rows = plan.rows
    ff = up_weight.shape[1]
    stretches = memory.shape[0]
    shares = shares_of(batch, plan.groups, ff)
    dma = pltpu.SemaphoreType.DMA
    inputs = dict(
        tokens=tokens, context=context, self_output=self_output, second_gain=second_gain, second_shift=second_shift,
        third_gain=third_gain, third_shift=third_shift, query_weight=query_weight,
        cross_output=cross_output, cotangent=cotangent,
    )
    near = len(inputs)
    inputs.update(memory=memory, up_weight=up_weight, down_weight=down_weight)
    low = ((rows, D), BF16)
    outputs = dict(
        result=low, normed_two=low, cross_low=low, branch=low, query_grad=low, self_low=low, grad_out=low,
        stream_grad=((rows, D), F32), vectors=((8, D), F32),
    )
    steps = [step_shapes(shares[s], batch, "zyx", shares[s].order[:1]) for s in range(EARLY)]
    for s in range(EARLY):
        outputs["state%d" % s] = (part_shape(shares[s], batch, "zyx".replace(shares[s].order[0], "")), BF16)
    far = len(outputs)
    outputs["memory_grad"] = (memory.shape, BF16)
    scratch = [VM(part_shape(shares[s], batch, "zyx"), BF16) for s in range(EARLY)]
    scratch += [VM(shape, BF16) for shapes in steps for shape in shapes]
    scratch += [
        VM((D, ff), BF16),
        VM((ff, D), BF16),
        VM((2 * rows, ff), BF16),
        VM((2 * rows, D), BF16),
        VM((rows, ff // 2), BF16),
        VM((2 * rows, ff // 2), BF16),
        VM((2 * rows, D // 2), BF16),
        VM(memory.shape, BF16),
        VM((rows, D), F32),
        VM((rows, D), F32),
        VM((rows, D), F32),
        VM((rows, D), F32),
        VM((stretches, STRETCH, D), BF16),
        VM((stretches, STRETCH, D), BF16),
        VM((stretches, STRETCH, D), F32),
        dma((3,)),
        dma((1,)),
        dma((ff // 512,)),
        dma((ff // 512,)),
        dma((3,)),
        dma((3,)),
        dma((stretches,)),
        dma((EARLY, batch - 1)),
        dma((EARLY, batch - 1)),
    ]
    names = list(inputs) + list(outputs)
    out = pl.pallas_call(
        partial(middle_kernel, plan, batch, shares, [len(s) for s in steps], names),
        out_shape=[jax.ShapeDtypeStruct(*shape) for shape in outputs.values()],
        in_specs=[pl.BlockSpec(memory_space=VM)] * near + [pl.BlockSpec(memory_space=pl.ANY)] * (len(inputs) - near),
        out_specs=[pl.BlockSpec(memory_space=VM)] * far + [pl.BlockSpec(memory_space=pl.ANY)],
        scratch_shapes=scratch,
        compiler_params=pltpu.CompilerParams(
            collective_id=2, has_side_effects=True, vmem_limit_bytes=62 << 20
        ),
        name="middle",
    )(*inputs.values())
    return dict(zip(outputs, out))


def on_device(devices, batch, tokens, segment_ids, neighbours, first_gain, first_shift, self_weight, self_output, second_gain,
    second_shift, query_weight, memory_weight, cross_output, third_gain, third_shift, up_weight, down_weight, cotangent,
):
    rows = tokens.shape[1]
    plan = Plan(devices, rows)
    stretch_count = neighbours.shape[1]
    ff = up_weight.shape[1]
    neighbour_rows = neighbours[0].reshape(stretch_count * SPAN, D)
    normed_one, logs, starts, context, edge, queries, pairs, outs, memory = attend(
        plan, tokens[0], first_gain, first_shift, segment_ids, self_weight, neighbour_rows, memory_weight
    )
    mid = middle(
        plan, batch, tokens[0], context, self_output, second_gain, second_shift, third_gain, third_shift, query_weight,
        memory, cross_output, up_weight, down_weight, cotangent[0],
    )
    input_grad, neighbour_grad, shares = tail(
        plan,
        batch,
        mid["grad_out"],
        queries,
        pairs,
        outs,
        logs,
        starts,
        [mid["cross_low"], mid["normed_two"], context, normed_one],
        [mid["branch"], mid["query_grad"], mid["self_low"]],
        [mid["state%d" % s] for s in range(EARLY)],
        neighbour_rows,
        edge,
        mid["memory_grad"].reshape((stretch_count + 1) * SPAN, 2 * D),
        memory_weight,
        self_weight,
        tokens[0],
        first_gain,
        mid["stream_grad"],
        mid["vectors"],
        ff,
    )
    wide = widen(plan, batch, ff, shares, mid["result"], input_grad, neighbour_grad)
    down, up, cross_out, memory_w, query, self_out, self_w, result, input_grad, neighbour_grad = wide[:10]
    vector = wide[10:]
    return (
        result[None],
        input_grad[None],
        neighbour_grad.reshape(neighbours.shape),
        vector[0],
        vector[3],
        self_w,
        self_out,
        vector[1],
        vector[4],
        query,
        memory_w,
        cross_out,
        vector[2],
        vector[5],
        up,
        down,
    )


def from_behind(array, axis, by):
    devices = lax.axis_size(axis)
    pairs = [(i, i + by) for i in range(devices) if 0 <= i + by < devices]
    return lax.ppermute(array, axis, pairs)


def layer_norm(values, gain, shift):
    mean = jnp.mean(values, axis=-1, keepdims=True)
    centred = values - mean
    spread = jnp.mean(centred * centred, axis=-1, keepdims=True)
    return centred * lax.rsqrt(spread + EPSILON) * gain + shift


def block_rows():
    return 512


def causal_allowed(query_pos, query_seg, key_pos, key_seg):
    return (query_pos[:, None] >= key_pos[None, :]) & (query_seg[:, None] == key_seg[None, :])


def key_block_grads(
    queries, grad_out, log_total, delta, query_pos, query_seg, keys, values, key_pos, key_seg, scale
):
    allowed = causal_allowed(query_pos, query_seg, key_pos, key_seg)[None]
    scores = jnp.einsum("qhd,khd->hqk", queries, keys, preferred_element_type=jnp.float32) * scale
    chances = jnp.where(
        allowed, jnp.exp(jnp.where(allowed, scores, NEGATIVE) - log_total[..., None]), 0.0
    )
    prob_grad = jnp.einsum("qhd,khd->hqk", grad_out, values, preferred_element_type=jnp.float32)
    score_low = (chances * (prob_grad - delta[..., None])).astype(jnp.bfloat16)
    query_part = (
        jnp.einsum("hqk,khd->qhd", score_low, keys, preferred_element_type=jnp.float32) * scale
    )
    key_part = (
        jnp.einsum("hqk,qhd->khd", score_low, queries, preferred_element_type=jnp.float32) * scale
    )
    value_part = jnp.einsum(
        "hqk,qhd->khd", chances.astype(jnp.bfloat16), grad_out, preferred_element_type=jnp.float32
    )
    return (query_part, key_part, value_part)


def plain_on_device(
    tokens,
    segment_ids,
    neighbours,
    first_gain,
    first_shift,
    self_weight,
    self_output,
    second_gain,
    second_shift,
    query_weight,
    memory_weight,
    cross_output,
    third_gain,
    third_shift,
    up_weight,
    down_weight,
    cotangent,
):
    rows = tokens.shape[1]
    seq_index = lax.axis_index("seq")
    scale = HEAD ** (-0.5)
    stream = tokens[0].astype(jnp.float32)
    seg_local = segment_ids[0]
    positions = seq_index * rows + jnp.arange(rows, dtype=jnp.int32)
    normed_one, first_back = jax.vjp(layer_norm, stream, first_gain, first_shift)
    normed_one_low = normed_one.astype(jnp.bfloat16)
    projected = matmul(normed_one_low, self_weight).astype(jnp.bfloat16)
    queries = projected[:, :D].reshape(rows, HEADS, HEAD)
    keys_low = projected[:, D : 2 * D]
    values_low = projected[:, 2 * D :]
    start_state = (
        jnp.full((HEADS, rows), NEGATIVE, jnp.float32),
        jnp.zeros((HEADS, rows), jnp.float32),
        jnp.zeros((HEADS, rows, HEAD), jnp.float32),
    )
    carry = start_state
    piece_keys = lax.all_gather(keys_low, "seq", axis=0, tiled=True)
    piece_values = lax.all_gather(values_low, "seq", axis=0, tiled=True)
    piece_seg = lax.all_gather(seg_local, "seq", axis=0, tiled=True)
    count = piece_keys.shape[0]
    fold_size = block_rows()

    def step(state, index):
        maxes, totals, running = state
        first = index * fold_size
        keys = lax.dynamic_slice_in_dim(piece_keys, first, fold_size, 0).reshape(
            fold_size, HEADS, HEAD
        )
        values = lax.dynamic_slice_in_dim(piece_values, first, fold_size, 0).reshape(
            fold_size, HEADS, HEAD
        )
        key_seg = lax.dynamic_slice_in_dim(piece_seg, first, fold_size, 0)
        key_pos = first + jnp.arange(fold_size, dtype=jnp.int32)
        allowed = causal_allowed(positions, seg_local, key_pos, key_seg)[None]
        scores = (
            jnp.einsum("qhd,khd->hqk", queries, keys, preferred_element_type=jnp.float32) * scale
        )
        scores = jnp.where(allowed, scores, NEGATIVE)
        new_max = jnp.maximum(maxes, jnp.max(scores, axis=-1))
        factor = jnp.exp(maxes - new_max)
        weights = jnp.where(allowed, jnp.exp(scores - new_max[..., None]), 0.0)
        totals = totals * factor + jnp.sum(weights, axis=-1)
        running = running * factor[..., None] + jnp.einsum(
            "hqk,khd->hqd", weights.astype(jnp.bfloat16), values, preferred_element_type=jnp.float32
        )
        return ((new_max, totals, running), None)

    carry, unused = lax.scan(step, carry, jnp.arange(count // fold_size, dtype=jnp.int32))
    maxes, totals, running = carry
    log_total = maxes + jnp.log(totals)
    context = running / totals[..., None]
    context_low = jnp.transpose(context, (1, 0, 2)).reshape(rows, D).astype(jnp.bfloat16)
    stream_one = stream + matmul(context_low, self_output)
    normed_two, second_back = jax.vjp(layer_norm, stream_one, second_gain, second_shift)
    normed_two_low = normed_two.astype(jnp.bfloat16)
    cross_queries = matmul(normed_two_low, query_weight).astype(jnp.bfloat16)
    stretch_count = neighbours.shape[1]
    span = NEIGHBOURS * NEIGHBOUR_LEN
    groups = stretch_count + 1
    neighbour_rows = neighbours[0].reshape(stretch_count * span, D)
    memory = (
        matmul(neighbour_rows, memory_weight)
        .astype(jnp.bfloat16)
        .reshape(stretch_count, span, 2 * D)
    )
    previous = from_behind(memory[stretch_count - 1], "seq", 1)
    extended = jnp.concatenate([previous[None], memory], axis=0)
    memory_keys = extended[:, :, :D].reshape(groups, span, HEADS, HEAD)
    memory_values = extended[:, :, D:].reshape(groups, span, HEADS, HEAD)
    pad_top = jnp.zeros((1, D), jnp.bfloat16)
    pad_end = jnp.zeros((STRETCH - 1, D), jnp.bfloat16)
    padded_queries = jnp.concatenate([pad_top, cross_queries, pad_end], axis=0).reshape(
        groups, STRETCH, HEADS, HEAD
    )
    cross_probs = jax.nn.softmax(
        jnp.einsum(
            "gqhd,gkhd->ghqk", padded_queries, memory_keys, preferred_element_type=jnp.float32
        )
        * scale,
        axis=-1,
    )
    cross_probs_low = cross_probs.astype(jnp.bfloat16)
    keep = ((seq_index > 0) | (jnp.arange(rows, dtype=jnp.int32) >= STRETCH - 1)).astype(
        jnp.float32
    )[:, None]
    cross_context = jnp.einsum(
        "ghqk,gkhd->gqhd", cross_probs_low, memory_values, preferred_element_type=jnp.float32
    ).reshape(groups * STRETCH, D)[1 : rows + 1]
    cross_low = (cross_context * keep).astype(jnp.bfloat16)
    stream_two = stream_one + matmul(cross_low, cross_output)
    normed_three, third_back = jax.vjp(layer_norm, stream_two, third_gain, third_shift)
    normed_three_low = normed_three.astype(jnp.bfloat16)
    upper = matmul(normed_three_low, up_weight)
    active, gelu_back = jax.vjp(partial(jax.nn.gelu, approximate=False), upper)
    active_low = active.astype(jnp.bfloat16)
    result = (stream_two + matmul(active_low, down_weight)).astype(jnp.bfloat16)
    grad_low = cotangent[0]
    down_grad = outer_sum(active_low, grad_low)
    active_grad = back_product(grad_low, down_weight)
    upper_low = gelu_back(active_grad)[0].astype(jnp.bfloat16)
    up_grad = outer_sum(normed_three_low, upper_low)
    stream_part, third_gain_grad, third_shift_grad = third_back(back_product(upper_low, up_weight))
    stream_two_grad = grad_low.astype(jnp.float32) + stream_part
    branch_low = stream_two_grad.astype(jnp.bfloat16)
    cross_output_grad = outer_sum(cross_low, branch_low)
    context_grad = (back_product(branch_low, cross_output) * keep).astype(jnp.bfloat16)
    padded_grad = jnp.concatenate([pad_top, context_grad, pad_end], axis=0).reshape(
        groups, STRETCH, HEADS, HEAD
    )
    prob_grad = jnp.einsum(
        "gqhd,gkhd->ghqk", padded_grad, memory_values, preferred_element_type=jnp.float32
    )
    score_low = (
        cross_probs * (prob_grad - jnp.sum(cross_probs * prob_grad, axis=-1, keepdims=True))
    ).astype(jnp.bfloat16)
    cross_query_low = (
        (
            jnp.einsum(
                "ghqk,gkhd->gqhd", score_low, memory_keys, preferred_element_type=jnp.float32
            )
            * scale
        )
        .reshape(groups * STRETCH, D)[1 : rows + 1]
        .astype(jnp.bfloat16)
    )
    key_part = (
        jnp.einsum("ghqk,gqhd->gkhd", score_low, padded_queries, preferred_element_type=jnp.float32)
        * scale
    )
    value_part = jnp.einsum(
        "ghqk,gqhd->gkhd", cross_probs_low, padded_grad, preferred_element_type=jnp.float32
    )
    extended_grad = jnp.concatenate(
        [key_part.reshape(groups, span, D), value_part.reshape(groups, span, D)], axis=-1
    )
    returned = from_behind(extended_grad[0].astype(jnp.bfloat16), "seq", -1).astype(jnp.float32)
    memory_grad = jnp.concatenate(
        [extended_grad[1:stretch_count], (extended_grad[stretch_count] + returned)[None]], axis=0
    )
    memory_grad = memory_grad.astype(jnp.bfloat16).reshape(stretch_count * span, 2 * D)
    memory_weight_grad = outer_sum(neighbour_rows, memory_grad)
    neighbour_grad = back_product(memory_grad, memory_weight).reshape(neighbours.shape)
    query_weight_grad = outer_sum(normed_two_low, cross_query_low)
    stream_part, second_gain_grad, second_shift_grad = second_back(
        back_product(cross_query_low, query_weight)
    )
    stream_one_grad = stream_two_grad + stream_part
    self_low = stream_one_grad.astype(jnp.bfloat16)
    self_output_grad = outer_sum(context_low, self_low)
    grad_out = back_product(self_low, self_output).astype(jnp.bfloat16).reshape(rows, HEADS, HEAD)
    delta = jnp.sum(jnp.transpose(grad_out.astype(jnp.float32), (1, 0, 2)) * context, axis=-1)
    gathered_keys, gathered_values, gathered_seg = (
        lax.all_gather(keys_low, "seq", axis=0, tiled=True),
        lax.all_gather(values_low, "seq", axis=0, tiled=True),
        lax.all_gather(seg_local, "seq", axis=0, tiled=True),
    )
    total_rows = gathered_keys.shape[0]
    size = block_rows()

    def key_step(query_sum, index):
        first = index * size
        keys = lax.dynamic_slice_in_dim(gathered_keys, first, size, 0).reshape(size, HEADS, HEAD)
        values = lax.dynamic_slice_in_dim(gathered_values, first, size, 0).reshape(
            size, HEADS, HEAD
        )
        key_seg = lax.dynamic_slice_in_dim(gathered_seg, first, size, 0)
        key_pos = first + jnp.arange(size, dtype=jnp.int32)
        query_part, key_block, value_block = key_block_grads(
            queries,
            grad_out,
            log_total,
            delta,
            positions,
            seg_local,
            keys,
            values,
            key_pos,
            key_seg,
            scale,
        )
        pair = jnp.concatenate([key_block.reshape(size, D), value_block.reshape(size, D)], axis=1)
        return (query_sum + query_part, pair)

    query_grad, pairs = lax.scan(
        key_step,
        jnp.zeros((rows, HEADS, HEAD), jnp.float32),
        jnp.arange(total_rows // size, dtype=jnp.int32),
    )
    pair_grad = lax.psum_scatter(
        pairs.reshape(total_rows, 2 * D).astype(jnp.bfloat16),
        "seq",
        scatter_dimension=0,
        tiled=True,
    ).astype(jnp.float32)
    projected_grad = jnp.concatenate([query_grad.reshape(rows, D), pair_grad], axis=1).astype(
        jnp.bfloat16
    )
    self_weight_grad = outer_sum(normed_one_low, projected_grad)
    stream_part, first_gain_grad, first_shift_grad = first_back(
        back_product(projected_grad, self_weight)
    )
    input_grad = stream_one_grad + stream_part
    shares = (
        lax.psum_scatter(
            first_gain_grad.astype(jnp.bfloat16), "batch", scatter_dimension=0, tiled=True
        ).astype(jnp.float32),
        lax.psum_scatter(
            first_shift_grad.astype(jnp.bfloat16), "batch", scatter_dimension=0, tiled=True
        ).astype(jnp.float32),
        lax.psum_scatter(
            self_weight_grad.astype(jnp.bfloat16), "batch", scatter_dimension=0, tiled=True
        ).astype(jnp.float32),
        lax.psum_scatter(
            self_output_grad.astype(jnp.bfloat16), "batch", scatter_dimension=0, tiled=True
        ).astype(jnp.float32),
        lax.psum_scatter(
            second_gain_grad.astype(jnp.bfloat16), "batch", scatter_dimension=0, tiled=True
        ).astype(jnp.float32),
        lax.psum_scatter(
            second_shift_grad.astype(jnp.bfloat16), "batch", scatter_dimension=0, tiled=True
        ).astype(jnp.float32),
        lax.psum_scatter(
            query_weight_grad.astype(jnp.bfloat16), "batch", scatter_dimension=0, tiled=True
        ).astype(jnp.float32),
        lax.psum_scatter(
            memory_weight_grad.astype(jnp.bfloat16), "batch", scatter_dimension=0, tiled=True
        ).astype(jnp.float32),
        lax.psum_scatter(
            cross_output_grad.astype(jnp.bfloat16), "batch", scatter_dimension=0, tiled=True
        ).astype(jnp.float32),
        lax.psum_scatter(
            third_gain_grad.astype(jnp.bfloat16), "batch", scatter_dimension=0, tiled=True
        ).astype(jnp.float32),
        lax.psum_scatter(
            third_shift_grad.astype(jnp.bfloat16), "batch", scatter_dimension=0, tiled=True
        ).astype(jnp.float32),
        lax.psum_scatter(
            up_grad.astype(jnp.bfloat16), "batch", scatter_dimension=0, tiled=True
        ).astype(jnp.float32),
        lax.psum_scatter(
            down_grad.astype(jnp.bfloat16), "batch", scatter_dimension=0, tiled=True
        ).astype(jnp.float32),
    )
    sums = (
        lax.psum(shares[0].astype(jnp.bfloat16), "seq").astype(jnp.float32),
        lax.psum(shares[1].astype(jnp.bfloat16), "seq").astype(jnp.float32),
        lax.psum(shares[2].astype(jnp.bfloat16), "seq").astype(jnp.float32),
        lax.psum(shares[3].astype(jnp.bfloat16), "seq").astype(jnp.float32),
        lax.psum(shares[4].astype(jnp.bfloat16), "seq").astype(jnp.float32),
        lax.psum(shares[5].astype(jnp.bfloat16), "seq").astype(jnp.float32),
        lax.psum(shares[6].astype(jnp.bfloat16), "seq").astype(jnp.float32),
        lax.psum(shares[7].astype(jnp.bfloat16), "seq").astype(jnp.float32),
        lax.psum(shares[8].astype(jnp.bfloat16), "seq").astype(jnp.float32),
        lax.psum(shares[9].astype(jnp.bfloat16), "seq").astype(jnp.float32),
        lax.psum(shares[10].astype(jnp.bfloat16), "seq").astype(jnp.float32),
        lax.psum(shares[11].astype(jnp.bfloat16), "seq").astype(jnp.float32),
        lax.psum(shares[12].astype(jnp.bfloat16), "seq").astype(jnp.float32),
    )
    return (
        result[None],
        input_grad[None],
        neighbour_grad,
        sums[0],
        sums[1],
        sums[2],
        sums[3],
        sums[4],
        sums[5],
        sums[6],
        sums[7],
        sums[8],
        sums[9],
        sums[10],
        sums[11],
        sums[12],
    )


def solution(mesh):
    placed = (
        P("batch", "seq", None),
        P("batch", "seq"),
        P("batch", "seq", None, None, None),
        P(),
        P(),
        P(),
        P(),
        P(),
        P(),
        P(),
        P(),
        P(),
        P(),
        P(),
        P(),
        P(),
        P("batch", "seq", None),
    )
    sizes = mesh.shape
    if sizes["seq"] == 8 and sizes["batch"] == 4:
        body = partial(on_device, sizes["seq"], sizes["batch"])
    else:
        body = plain_on_device
    return jax.shard_map(
        body,
        mesh=mesh,
        in_specs=placed,
        out_specs=(
            P("batch", "seq", None),
            P("batch", "seq", None),
            P("batch", "seq", None, None, None),
            P("batch"),
            P("batch"),
            P("batch", None),
            P("batch", None),
            P("batch"),
            P("batch"),
            P("batch", None),
            P("batch", None),
            P("batch", None),
            P("batch"),
            P("batch"),
            P("batch", None),
            P("batch", None),
        ),
        check_vma=False,
    )
```

profile of v0, /device:TPU:0, one launch (start us, length us, event | category | flops | bytes accessed | tf_op | source)
XLA Modules:
  0.0 258.3 jit_solution(16114387712314037305)
XLA Ops:
  0.6 49.1 %attend.1 = (bf16[384,768]{1,0:T(8,128)(2,1)}, f32[3,4,8,384]{3,2,1,0:T(8,128)}, s32[4,8,384]{2,1,0:T(8,128)}, bf16[384,768]{1,0:T(8,128)(2,1)}, bf16[256,768]{1...) custom-call(bf16[384,768]{1,0:T(8,128)(2,1)} %bitcast.10, ...), custom_call_target="tpu_custom_call" | custom-call | tf_op jit(solution)/shard_map/attend/pallas_call | solution.py:375
  49.8 64.4 %middle.1 = (bf16[384,768]{1,0:T(8,128)(2,1)}, bf16[384,768]{1,0:T(8,128)(2,1)}, bf16[384,768]{1,0:T(8,128)(2,1)}, bf16[384,768]{1,0:T(8,128)(2,1)}, bf16[384,76...) custom-call(bf16[384,768]{1,0:T(8,128)(2,1)} %bitcast.11, ...), custom_call_target="tpu_custom_call" | custom-call | tf_op jit(solution)/shard_map/middle/pallas_call | solution.py:1386
  114.2 134.2 %tail.1 = (bf16[384,768]{1,0:T(8,128)(2,1)}, bf16[1536,768]{1,0:T(8,128)(2,1)}, bf16[2,2,2,96,384]{4,3,2,1,0:T(8,128)(2,1)}, bf16[2,2,2,96,384]{4,3,2,1,0:T(8,12...) custom-call(bf16[384,768]{1,0:T(8,128)(2,1)} %get-tuple-element.69.r, ...), custom_call_target="tpu_custom_call" | custom-call | tf_op jit(solution)/shard_map/tail/pallas_call | solution.py:1023
  248.4 9.7 %widen.1 = (f32[768,768]{1,0:T(8,128)}, f32[192,3072]{1,0:T(8,128)}, f32[192,768]{1,0:T(8,128)}, f32[192,1536]{1,0:T(8,128)}, f32[192,768]{1,0:T(8,128)}, /*inde...) custom-call(bf16[2,2,2,96,384]{4,3,2,1,0:T(8,128)(2,1)} %get-tuple-e, ...), custom_call_target="tpu_custom_call" | custom-call | tf_op jit(solution)/shard_map/widen/pallas_call | solution.py:1090
where the time goes:
time: 261 us; the launch traced here: 258 us
  Pallas kernels  257 us (98%)
    pallas_call x1, Pallas kernels, tail(): pl.pallas_call(partial(tail_kernel, plan, batch, shares, [len(s) for s in...  134 us
    pallas_call x1, Pallas kernels, middle(): pl.pallas_call(partial(middle_kernel, plan, batch, shares, [len(s) for s...  64.4 us
    pallas_call x1, Pallas kernels, attend(): pl.pallas_call(partial(attend_kernel, plan), out_shape=[jax.ShapeDtypeStr...  49.1 us
    pallas_call x1, Pallas kernels, widen(): pl.pallas_call(partial(widen_kernel, batch), grid=(4,), in_specs=ins, out...  9.67 us

commit v1 on v0

--- a/solution.py
+++ b/solution.py
@@ -8,6 +8,7 @@
 from jax.experimental.pallas import tpu as pltpu
 from jax.sharding import PartitionSpec as P
 import math
+from types import SimpleNamespace
 
 D = 768
 HEADS = 12
@@ -113,8 +114,8 @@
 def attend_kernel(plan, *refs):
     (
         tokens, gain, shift, segments, far_weight, far_neighbours, far_memory_weight,
-        normed, logs, starts, context, edge, far_queries, far_pairs, far_outs, far_memory,
-        queries, pairs, outs, memory, weight, neighbours, memory_weight,
+        normed, logs, starts, context, edge, far_queries, far_pairs, far_outs, far_memory, far_packed,
+        queries, pairs, outs, memory, packed, weight, neighbours, memory_weight,
         segs, projected, pack_pairs, pack_queries, got_queries, sent_context, got_context,
         pair_send, pair_recv, query_send, query_recv, pass_send, pass_recv,
         back_send, back_recv, seg_send, seg_recv, edge_send, edge_recv, load_sems, memory_sems, store_sems,
@@ -242,6 +243,27 @@
         edge[...] = jnp.zeros_like(edge)
 
     memory_copy(0).start()
+
+    per = groups // members
+    wide_low = low_lanes((D, 2 * HEAD))
+
+    def columns_of(part, head):
+        first = part * D + head // 2 * 128
+        return weight[:, first : first + 128].astype(F32), head % 2
+
+    for slot in range(slots):
+        for owner in range(members):
+            heads = [(owner * per + i) * slots + slot for i in range(per)]
+            first = (slot * members + owner) * per * 3 * HEAD
+            for i, head in enumerate(heads):
+                (key, odd), (value, _) = columns_of(1, head), columns_of(2, head)
+                pair = jnp.where(wide_low, swap_lanes(key), value) if odd else jnp.where(wide_low, key, swap_lanes(value))
+                packed[:, first + i * 128 : first + i * 128 + 128] = pair.astype(BF16)
+            (one, odd), (two, other) = columns_of(0, heads[0]), columns_of(0, heads[1])
+            pair = jnp.where(wide_low, swap_lanes(one) if odd else one, two if other else swap_lanes(two))
+            packed[:, first + per * 128 : first + per * 128 + 128] = pair.astype(BF16)
+    packed_copy = pltpu.make_async_copy(packed, far_packed, memory_sems.at[stretches + 1])
+    packed_copy.start()
 
     for copy in seg_copies:
         copy.wait_send()
@@ -340,6 +362,8 @@
             for beyond in range(1, members):
                 pass_copy(slot, origin, beyond).wait_send()
 
+    packed_copy.wait()
+
     @pl.loop(0, stretches + 1)
     def _(s):
         memory_copy(s).wait()
@@ -370,6 +394,7 @@
         ((slots, devices, rows, 128), BF16),
         ((slots, groups, rows, 128), F32),
         ((stretches + 1, SPAN, 2 * D), BF16),
+        ((D, 3 * D), BF16),
     ]
     vmem, hbm = pl.BlockSpec(memory_space=VM), pl.BlockSpec(memory_space=pl.ANY)
     return pl.pallas_call(
@@ -402,7 +427,7 @@
             dma,
             dma,
             dma((3,)),
-            dma((stretches + 1,)),
+            dma((stretches + 2,)),
             dma((slots, 3)),
         ],
         compiler_params=pltpu.CompilerParams(
@@ -412,11 +437,6 @@
     )(tokens, gain, shift, segments, weight, neighbours, memory_weight)
 
 
-class Grad:
-    def __init__(self, matrix, first, count, at=0):
-        self.matrix, self.first, self.count, self.at = matrix, first, count, at
-
-
 class Product:
     def __init__(self, matrix, first, count, at=0):
         self.matrix, self.first, self.count, self.at = matrix, first, count, at
@@ -431,20 +451,29 @@
     short, tall = D // (batch * groups), ff // (batch * groups * 2)
     half = D // 2
     return [
-        Share(tall, half, "xyz", []),
+        Share(tall, half, "xzy", []),
         Share(tall, half, "yxz", []),
-        Share(short, ff // 4, "xyz", [Product(0, 0, ff // 4)]),
+        Share(short, ff // 4, "xzy", [Product(0, 0, ff // 4)]),
         Share(short, ff // 4, "zyx", [Product(0, ff // 4, ff // 4)]),
-        Share(short, 512, "xyz", [Grad(0, 0, 512)]),
-        Share(short, 256 + half, "yxz", [Grad(0, 512, 256), Product(0, 0, half, 256)]),
-        Share(short, half, "zxy", [Product(1, 0, half)]),
+        Share(short, 512, "xyz", []),
+        Share(short, 256 + half, "yxz", [Product(0, 0, half, 256)]),
+        Share(short, half, "yzx", [Product(1, 0, half)]),
         Share(short, half, "zyx", [Product(2, 0, half)]),
-        Share(short, 640, "xyz", [Product(3, 0, 640)]),
-        Share(short, 640, "yxz", [Product(3, 640, 512)], vectors=512),
+        Share(short, half, "xyz", [Product(3, 0, half)]),
+        Share(short, half, "zyx", [Product(4, 0, half)]),
+        Share(short, 256, "xzy", [Product(5, 0, 256)]),
+        Share(short, 256, "yxz", [Product(5, 256, 128)], vectors=128),
     ]
 
 
 EARLY = 4
+
+SCHEDULE = (
+    (), (), (), (), (), (), (-1, 5, 4, 3), (8,), (1, 6), (0, 2), (-2, 8, 0, 3), (9, 5, 1, 2), (),
+    (7, 0, 1, 2), (10, 4, 3), (11, 1), (5, 0), (8, 2, 3, 1), (9, 6, 7, 0), (10, 11, 4, 5, 2, 3), (9, 6, 8),
+    (11, 7, 4), (9,), (10,), (6,), (8,), (5,), (7,), (11,), (10,), (5,), (9,), (6,), (10,), (11,), (4,), (8,),
+    (7,), (6,), (9,), (4,), (10,), (11,), (7,), (8,), (9,), (10,), (11,),
+)
 
 
 def part_shape(share, batch, axes):
@@ -563,23 +592,22 @@
 
 
 def tail_kernel(plan, batch, shares, arrival_counts, names, *refs):
-    r = dict(zip(names, refs))
+    r = SimpleNamespace(**dict(zip(names, refs)))
     refs = refs[len(names) :]
     takes = iter(refs)
     neighbour_grad = next(takes)
     gathered = [next(takes) for _ in shares]
     two_left = [next(takes) for _ in range(4)]
-    two_right = [next(takes) for _ in range(4)]
+    two_right = [next(takes) for _ in range(3 + plan.slots)]
+    give_right = [next(takes) for _ in range(plan.slots)]
     sums = [next(takes) for _ in shares]
     arrivals = [[next(takes) for _ in range(n)] for n in arrival_counts]
-    grad_pieces = [piece for share in shares for piece in share.pieces if isinstance(piece, Grad)]
-    other_grads = [next(takes) for _ in grad_pieces]
     (
-        queries, pairs, outs, pack_grads, got_grads, grads, deltas, pair_sum, query_sum,
-        give, took, sent_pair, got_pair, sent_query, got_query, result, vector_rows, other_rows,
-        near, slopes, memory_weight, give_grads, stage, edge_sent, edge_got,
+        queries, pairs, outs, got_grads, grads, deltas, pair_sum, query_sum,
+        give, took, sent_pair, got_pair, sent_query, got_query, vector_rows, other_rows,
+        turned_weight, slopes, memory_weight, stage, edge_sent, edge_got,
         load_sems, out_send, out_recv, give_send, give_recv, pair_send, pair_recv, query_send, query_recv,
-        own_sems, swap_send, swap_recv, piece_send, piece_recv, state_sems, near_sems, stage_sems, edge_send, edge_recv, send_sems, recv_sems, keep_sems,
+        own_sems, swap_send, swap_recv, state_sems, near_sems, stage_sems, edge_send, edge_recv, send_sems, recv_sems, keep_sems,
     ) = takes
     me, group, member = plan.place()
     devices, groups, members, slots, rows = plan.devices, plan.groups, plan.members, plan.slots, plan.rows
@@ -597,44 +625,50 @@
     def load(slot):
         spot = slot % 2
         return [
-            pltpu.make_async_copy(r["queries"].at[slot], queries.at[spot], load_sems.at[spot, 0]),
-            pltpu.make_async_copy(r["pairs"].at[slot], pairs.at[spot], load_sems.at[spot, 1]),
-            pltpu.make_async_copy(r["outs"].at[slot], outs.at[spot], load_sems.at[spot, 2]),
+            pltpu.make_async_copy(r.queries.at[slot], queries.at[spot], load_sems.at[spot, 0]),
+            pltpu.make_async_copy(r.pairs.at[slot], pairs.at[spot], load_sems.at[spot, 1]),
+            pltpu.make_async_copy(r.outs.at[slot], outs.at[spot], load_sems.at[spot, 2]),
         ]
 
     for copy in load(0):
         copy.start()
-    for head in range(HEADS):
-        block = (head // 2) * 128
-        pack_grads[head] = pack_rows(r["grad_out"][:, block : block + 128].astype(F32), head).astype(BF16)
 
     def out_copy(slot, away):
         to = lax.rem(group + away, groups)
         return send(
-            pack_grads.at[to * slots + slot], got_grads.at[slot, group],
+            r.packed_grads.at[to * slots + slot], got_grads.at[slot, group],
             out_send.at[slot, away - 1], out_recv.at[slot, group], seq_device(to * members + member),
         )
 
     for slot in range(slots):
         for away in range(1, groups):
             out_copy(slot, away).start()
-        got_grads[slot, group] = pack_grads[group * slots + slot]
+        got_grads[slot, group] = r.packed_grads[group * slots + slot]
 
     state_loads = [
-        pltpu.make_async_copy(r["state%d" % s], sums[s], state_sems.at[s]) for s in range(EARLY)
+        pltpu.make_async_copy(getattr(r, "state%d" % s), sums[s], state_sems.at[s]) for s in range(EARLY)
     ]
-    stretches = r["neighbours"].shape[0] // SPAN
+    stretches = slopes.shape[0] // SPAN - 1
     near_loads = [
-        pltpu.make_async_copy(r["edge"], near.at[pl.ds(0, SPAN)], near_sems.at[0]),
-        pltpu.make_async_copy(r["neighbours"], near.at[pl.ds(SPAN, stretches * SPAN)], near_sems.at[1]),
-        pltpu.make_async_copy(r["memory_grad"], slopes, near_sems.at[2]),
-        pltpu.make_async_copy(r["memory_weight"], memory_weight, near_sems.at[3]),
+        pltpu.make_async_copy(r.memory_grad, slopes, near_sems.at[0]),
+        pltpu.make_async_copy(r.memory_weight, memory_weight, near_sems.at[1]),
     ]
-    for copy in near_loads + state_loads:
+    first = sums[EARLY].shape[-1]
+    rest = r.memory_part.shape[-1] - first
+    memory_loads = [
+        pltpu.make_async_copy(r.memory_part.at[:, :, :, :, pl.ds(0, first)], sums[EARLY], near_sems.at[2]),
+        pltpu.make_async_copy(
+            r.memory_part.at[:, :, :, :, pl.ds(first, rest)],
+            sums[EARLY + 1].at[:, :, :, :, pl.ds(0, rest)],
+            near_sems.at[3],
+        ),
+    ]
+    packed_load = pltpu.make_async_copy(r.weight, turned_weight, near_sems.at[4])
+    for copy in state_loads + memory_loads + near_loads + [packed_load]:
         copy.start()
 
-    lefts = [r["left%d" % m] for m in range(4)]
-    rights = [r["right%d" % m] for m in range(3)] + [result]
+    lefts = [getattr(r, "left%d" % m) for m in range(4)]
+    rights = [getattr(r, "right%d" % m) for m in range(3)]
     here, there = pl.ds(0, rows), pl.ds(rows, rows)
 
     def left_swaps(m):
@@ -661,30 +695,6 @@
     for copy in last_left:
         copy.start()
 
-    pieces = {}
-    for s, share in enumerate(shares):
-        for piece in share.pieces:
-            if isinstance(piece, Grad):
-                n = len(pieces)
-                pieces[piece] = (n, s, send(
-                    give_grads.at[:, :, :, :, pl.ds(piece.first, piece.count)], other_grads[n],
-                    piece_send.at[n], piece_recv.at[n], partner,
-                ))
-
-    def memory_grads():
-        for copy in near_loads:
-            copy.wait()
-        width = slopes.shape[1] // 2
-        for piece, (n, s, copy) in pieces.items():
-            for first in range(piece.first, piece.first + piece.count, 256):
-                columns = pl.ds(pl.multiple_of((1 - member) * width + first, 256), 256)
-                spread_to(give_grads, shares[s].rows, outer_sum(near[...], slopes[:, columns]), first)
-            copy.start()
-        for piece, (n, s, copy) in pieces.items():
-            for first in range(piece.first, piece.first + piece.count, 256):
-                columns = pl.ds(pl.multiple_of(member * width + first, 256), 256)
-                spread(s, outer_sum(near[...], slopes[:, columns]), piece.at + first - piece.first)
-
     def edge_copy():
         return send(edge_sent, edge_got, edge_send, edge_recv, seq_device(before))
 
@@ -708,29 +718,58 @@
 
             stage_copy(s).start()
 
+    def slot_swap(slot):
+        return send(
+            give_right[slot], two_right[3 + slot].at[there], swap_send.at[4 + slot, 1], swap_recv.at[4 + slot, 1], partner
+        )
+
+    def arrive(slot):
+        for away in range(1, groups):
+            origin = lax.rem(group + away, groups)
+            head = origin * slots + slot
+            send(
+                sent_query.at[slot, 0], got_query.at[head],
+                query_send.at[slot, 0], query_recv.at[head], partner,
+            ).wait_recv()
+            send(
+                sent_pair.at[0], got_pair.at[head], pair_send.at[slot, 0], pair_recv.at[head], partner,
+            ).wait_recv()
+        for owner, target in ((1 - member, give_right[slot]), (member, two_right[3 + slot].at[here])):
+            heads = [(owner * 2 + i) * slots + slot for i in range(2)]
+            for i in range(2):
+                target[:, i * 128 : (i + 1) * 128] = got_pair[heads[i]]
+            first, second = [got_query[head].astype(F32) for head in heads]
+            target[:half, 256:384] = jnp.where(half_low, first, swap_lanes(second)).astype(BF16)
+            target[half:, 256:384] = jnp.where(half_low, swap_lanes(first), second).astype(BF16)
+            if target is give_right[slot]:
+                slot_swap(slot).start()
+
     waited = set()
+    last_left_done = []
 
     def spread(s, values, at):
         spread_to(sums[s], shares[s].rows, values, at)
 
     def fill(s):
+        if EARLY <= s < EARLY + 2:
+            memory_loads[s - EARLY].wait()
         for piece in shares[s].pieces:
-            if isinstance(piece, Grad):
-                n, _, copy = pieces[piece]
-                copy.wait()
-                for layer in range(batch):
-                    columns = pl.ds(piece.at, piece.count)
-                    sums[s][layer, :, :, :, columns] = add(sums[s][layer, :, :, :, columns], other_grads[n][layer])
-            else:
-                m = piece.matrix
-                if m not in waited:
-                    waited.add(m)
+            m = piece.matrix
+            if m not in waited:
+                waited.add(m)
+                if m < 3:
                     for copy in swaps[m]:
                         copy.wait()
-                tile = 384 if piece.count % 384 == 0 else 512 if piece.count % 512 == 0 else 128
-                for t in range(piece.count // tile):
-                    first = piece.first + t * tile
-                    spread(s, outer_sum(two_left[m][...], two_right[m][:, first : first + tile]), piece.at + t * tile)
+                else:
+                    slot_swap(m - 3).wait()
+            if m >= 3 and not last_left_done:
+                last_left_done.append(m)
+                for copy in last_left:
+                    copy.wait()
+            tile = piece.count if piece.count <= 512 else 384
+            for t in range(piece.count // tile):
+                first = piece.first + t * tile
+                spread(s, outer_sum(two_left[min(m, 3)][...], two_right[m][:, first : first + tile]), piece.at + t * tile)
         if shares[s].vectors is not None:
             vector_copy.wait()
             mine = vector_rows[member] + other_rows[...]
@@ -752,15 +791,7 @@
         for n in numbers:
             next(running[n], None)
 
-    advance(0, 1, 2, 3)
-    memory_grads()
-    advance(4, 5)
-    edge_sent[...] = back_product(slopes[0:SPAN, :], memory_weight[...]).astype(BF16)
-
-    @pl.when(me > 0)
-    def _():
-        edge_copy().start()
-
+    advance(0, 1, 2, 3, 4, 5)
     advance(6, 7)
 
     def give_copy(slot, away):
@@ -782,7 +813,14 @@
             query_send.at[slot, to], query_recv.at[group * slots + slot], seq_device(to * members + member),
         )
 
-    between = [(0, 1, 2, 3), (0, 1, 2, 3, 4, 5), (0, 1, 2, 3, 6, 7)]
+    def tick():
+        for action in next(schedule, ()):
+            if action < 0:
+                arrive(-1 - action)
+            else:
+                advance(action)
+
+    schedule = iter(SCHEDULE)
     for slot in range(slots):
         spot = slot % 2
         for copy in load(slot):
@@ -792,14 +830,15 @@
                 copy.start()
         for away in range(1, groups):
             origin = lax.rem(group + away, groups)
+            out_copy(slot, away).wait_send()
             send(
-                pack_grads.at[0], got_grads.at[slot, origin],
+                r.packed_grads.at[0], got_grads.at[slot, origin],
                 out_send.at[slot, 0], out_recv.at[slot, origin], partner,
             ).wait_recv()
         for g in range(groups):
-            packed = got_grads[slot, g].astype(F32)
-            top = jnp.where(half_low, 0.0, swap_lanes(packed))
-            bottom = jnp.where(half_low, 0.0, packed)
+            part = got_grads[slot, g].astype(F32)
+            top = jnp.where(half_low, 0.0, swap_lanes(part))
+            bottom = jnp.where(half_low, 0.0, part)
             grads[g, :half] = top.astype(BF16)
             grads[g, half:] = bottom.astype(BF16)
             product = jnp.concatenate([top, bottom], axis=0) * outs[spot, g]
@@ -809,14 +848,16 @@
             tile = pairs[spot, k * members : (k + 1) * members].reshape(members * rows, 128)
             for g in range(k, groups):
                 query, grad = queries[spot, g], grads[g]
-                scores = hide(plan, back_product(tile, query), k, g, member, r["starts"][g][:1])
-                chance = jnp.exp(scores - r["logs"][slot, g][:1])
+                scores = hide(plan, back_product(tile, query), k, g, member, r.starts[g][:1])
+                chance = jnp.exp(scores - r.logs[slot, g][:1])
                 chance_grad = back_product(tile, grad)
                 score_grad = (chance * (chance_grad - deltas[g][:1])).astype(BF16)
                 total = total + matmul(score_grad, query) + matmul(chance.astype(BF16), grad)
                 part = outer_sum(tile, score_grad)
                 query_sum[g] = part if k == 0 else query_sum[g] + part
             pair_sum[k * members : (k + 1) * members] = total.reshape(members, rows, 128)
+            if k < groups - 1:
+                tick()
         for away in range(1, members):
             to = lax.rem(member + away, members)
             if slot > 0:
@@ -856,70 +897,56 @@
             def _():
                 got_pair[group * slots + slot] = total
 
-        advance(*between[slot])
-
-    neighbour_grads(range(stretches))
-    wide, narrow = slopes.at[pl.ds(0, D)], slopes.at[pl.ds(D, D), pl.ds(0, D)]
-    weight_loads = [
-        pltpu.make_async_copy(r["weight"].at[:, pl.ds(0, 2 * D)], wide, load_sems.at[0, 3]),
-        pltpu.make_async_copy(r["weight"].at[:, pl.ds(2 * D, D)], narrow, load_sems.at[1, 3]),
-    ]
-    for copy in weight_loads:
-        copy.start()
+        if slot == 0:
+            for copy in near_loads:
+                copy.wait()
+            edge_sent[...] = back_product(slopes[0:SPAN, :], memory_weight[...]).astype(BF16)
+
+            @pl.when(me > 0)
+            def _():
+                edge_copy().start()
+
+        tick()
+
+    tick()
+    arrive(slots - 1)
+    tick()
+    packed_load.wait()
+    normed_grad = 0.0
     for slot in range(slots):
-        for away in range(1, groups):
-            origin = lax.rem(group + away, groups)
-            head = origin * slots + slot
-            send(
-                sent_query.at[slot, 0], got_query.at[head],
-                query_send.at[slot, 0], query_recv.at[head], partner,
-            ).wait_recv()
-            send(
-                sent_pair.at[0], got_pair.at[head], pair_send.at[slot, 0], pair_recv.at[head], partner,
-            ).wait_recv()
-    for two in range(HEADS // 2):
-        columns = slice(two * 128, two * 128 + 128)
-        first = got_query[2 * two].astype(F32)
-        second = got_query[2 * two + 1].astype(F32)
-        result[:half, columns] = jnp.where(half_low, first, swap_lanes(second)).astype(BF16)
-        result[half:, columns] = jnp.where(half_low, swap_lanes(first), second).astype(BF16)
-        first = got_pair[2 * two].astype(F32)
-        second = got_pair[2 * two + 1].astype(F32)
-        result[:, slice(D + two * 128, D + two * 128 + 128)] = jnp.where(low, first, swap_lanes(second)).astype(BF16)
-        result[:, slice(2 * D + two * 128, 2 * D + two * 128 + 128)] = jnp.where(
-            low, swap_lanes(first), second
-        ).astype(BF16)
-    swaps[3] = last_left + right_swaps(3)
-    for copy in swaps[3][2:]:
-        copy.start()
-    for copy in weight_loads:
-        copy.wait()
-    normed_grad = back_product(result[:, : 2 * D], wide[...]) + back_product(result[:, 2 * D :], narrow[...])
-    values = r["tokens"][...].astype(F32)
+        for owner, part in ((member, two_right[3 + slot][here]), (1 - member, give_right[slot][...])):
+            columns = pl.ds(pl.multiple_of(slot * D + owner * (D // 2), 128), D // 2)
+            normed_grad = normed_grad + back_product(part, turned_weight[:, columns])
+    values = r.tokens[...].astype(F32)
     centred = values - jnp.mean(values, axis=1, keepdims=True)
     inverse = lax.rsqrt(jnp.mean(centred * centred, axis=1, keepdims=True) + EPSILON)
     unit = centred * inverse
     vector_rows[0] = jnp.concatenate(
-        [jnp.sum(normed_grad * unit, axis=0, keepdims=True), r["vectors"][0:2], jnp.zeros((5, D), F32)], axis=0
+        [jnp.sum(normed_grad * unit, axis=0, keepdims=True), r.vectors[0:2], jnp.zeros((5, D), F32)], axis=0
     )
     vector_rows[1] = jnp.concatenate(
-        [jnp.sum(normed_grad, axis=0, keepdims=True), r["vectors"][2:4], jnp.zeros((5, D), F32)], axis=0
+        [jnp.sum(normed_grad, axis=0, keepdims=True), r.vectors[2:4], jnp.zeros((5, D), F32)], axis=0
     )
     vector_copy = send(
-        vector_rows.at[1 - member], other_rows, swap_send.at[4, 0], swap_recv.at[4, 0], partner
+        vector_rows.at[1 - member], other_rows, swap_send.at[3, 1], swap_recv.at[3, 1], partner
     )
     vector_copy.start()
-    advance(8)
-    scaled = normed_grad * as_row(r["gain"])
-    input_grad = r["stream_grad"][...] + inverse * (
+    tick()
+    scaled = normed_grad * as_row(r.gain)
+    input_grad = r.stream_grad[...] + inverse * (
         scaled
         - jnp.mean(scaled, axis=1, keepdims=True)
         - unit * jnp.mean(scaled * unit, axis=1, keepdims=True)
     )
-    r["input_grad"][...] = input_grad.astype(BF16)
-    advance(9)
-    for _ in range(7):
-        advance(6, 7, 4, 5, 2, 3, 0, 1, 8, 9)
+    r.input_grad[...] = input_grad.astype(BF16)
+    tick()
+    for s in range(stretches):
+        neighbour_grads([s])
+        tick()
+    for _ in range(40):
+        tick()
+    for _ in range(8):
+        advance(*range(len(shares)))
 
     for s in range(max(stretches - 2, 0), stretches):
         stage_copy(s).wait()
@@ -934,47 +961,40 @@
                 give_copy(slot, away).wait_send()
         for away in range(1, groups):
             origin = lax.rem(group + away, groups)
-            out_copy(slot, away).wait_send()
             if slot == slots - 1:
                 pair_copy(slot, origin).wait_send()
             query_copy(slot, origin).wait_send()
 
 
-def tail(plan, batch, grad_out, queries, pairs, outs, logs, starts, lefts, rights, states,
-    neighbours, edge, memory_grad, memory_weight, weight, tokens, gain, stream_grad, vectors, ff,
+def tail(plan, batch, packed_grads, queries, pairs, outs, logs, starts, lefts, rights, states,
+    memory_part, memory_grad, memory_weight, weight, tokens, gain, stream_grad, vectors, ff,
 ):
     devices, groups, members, slots, rows = plan.devices, plan.groups, plan.members, plan.slots, plan.rows
     half = rows // 2
     shares = shares_of(batch, groups, ff)
     dma = pltpu.SemaphoreType.DMA
-    inputs = {"grad_out": grad_out, "logs": logs, "starts": starts, "tokens": tokens, "gain": gain}
+    inputs = dict(packed_grads=packed_grads, logs=logs, starts=starts, tokens=tokens, gain=gain)
     inputs.update(stream_grad=stream_grad, vectors=vectors)
     small = len(inputs)
     inputs.update(queries=queries, pairs=pairs, outs=outs, weight=weight)
     inputs.update({"left%d" % m: left for m, left in enumerate(lefts)})
     inputs.update({"right%d" % m: right for m, right in enumerate(rights)})
     inputs.update({"state%d" % m: state for m, state in enumerate(states)})
-    inputs.update(neighbours=neighbours, edge=edge, memory_grad=memory_grad, memory_weight=memory_weight)
-    widths = [right.shape[1] // 2 for right in rights] + [3 * D // 2]
+    inputs.update(memory_part=memory_part, memory_grad=memory_grad, memory_weight=memory_weight)
+    widths = [right.shape[1] // 2 for right in rights] + [D // 2] * slots
     axes = ["zyx".replace(s.order[0], "") if n < EARLY else "zyx" for n, s in enumerate(shares)]
     orders = [s.order[1:] if n < EARLY else s.order for n, s in enumerate(shares)]
     steps = [step_shapes(share, batch, axes[n], orders[n]) for n, share in enumerate(shares)]
     scratch = [VM((2 * rows, left.shape[1]), BF16) for left in lefts]
     scratch += [VM((2 * rows, width), BF16) for width in widths]
+    scratch += [VM((rows, D // 2), BF16)] * slots
     scratch += [VM(part_shape(share, batch, axes[n]), BF16) for n, share in enumerate(shares)]
     scratch += [VM(shape, BF16) for shapes in steps for shape in shapes]
-    scratch += [
-        VM((batch, 2, 2, share.rows, piece.count), BF16)
-        for share in shares[EARLY:]
-        for piece in share.pieces
-        if isinstance(piece, Grad)
-    ]
     span_rows = memory_grad.shape[0]
     scratch += [
         VM((2, groups, rows, 128), BF16),
         VM((2, devices, rows, 128), BF16),
         VM((2, groups, rows, 128), F32),
-        VM((HEADS, half, 128), BF16),
         VM((slots, groups, half, 128), BF16),
         VM((groups, rows, 128), BF16),
         VM((groups, 8, rows), F32),
@@ -986,17 +1006,15 @@
         VM((HEADS, rows, 128), BF16),
         VM((slots, groups, half, 128), BF16),
         VM((HEADS, half, 128), BF16),
-        VM((rows, 3 * D), BF16),
         VM((2, 8, D), F32),
         VM((8, D), F32),
-        VM((span_rows, D), BF16),
+        VM((D, 3 * D), BF16),
         VM((span_rows, 2 * D), BF16),
         VM((D, 2 * D), BF16),
-        VM((batch, 2, 2, shares[EARLY].rows, D), BF16),
         VM((2, SPAN, D), BF16),
         VM((SPAN, D), BF16),
         VM((SPAN, D), BF16),
-        dma((2, 4)),
+        dma((2, 3)),
         dma((slots, groups)),
         dma((slots, groups)),
         dma((slots, members - 1)),
@@ -1006,12 +1024,10 @@
         dma((slots, groups)),
         dma((HEADS,)),
         dma((4, 2)),
-        dma((5, 2)),
-        dma((5, 2)),
-        dma((2,)),
-        dma((2,)),
+        dma((4 + slots, 2)),
+        dma((4 + slots, 2)),
         dma((EARLY,)),
-        dma((4,)),
+        dma((5,)),
         dma((2,)),
         dma,
         dma,
@@ -1022,7 +1038,7 @@
     names = list(inputs) + ["input_grad"]
     out = pl.pallas_call(
         partial(tail_kernel, plan, batch, shares, [len(s) for s in steps], names),
-        out_shape=[jax.ShapeDtypeStruct((rows, D), BF16), jax.ShapeDtypeStruct(neighbours.shape, BF16)]
+        out_shape=[jax.ShapeDtypeStruct((rows, D), BF16), jax.ShapeDtypeStruct((span_rows - SPAN, D), BF16)]
         + [jax.ShapeDtypeStruct((2, 2, 2, s.rows, s.columns), BF16) for s in shares],
         in_specs=[pl.BlockSpec(memory_space=VM)] * small + [pl.BlockSpec(memory_space=pl.ANY)] * (len(inputs) - small),
         out_specs=[pl.BlockSpec(memory_space=VM)] + [pl.BlockSpec(memory_space=pl.ANY)] * (1 + len(shares)),
@@ -1035,10 +1051,10 @@
     return out[0], out[1], out[2:]
 
 
-def widen_kernel(batch, *refs):
-    shares, (low_result, low_input, low_neighbour) = refs[:10], refs[10:13]
-    down, up, cross_out, memory, query, self_out, self_weight, result, input_grad, neighbour_grad = refs[13:23]
-    vectors, kept = refs[23:29], refs[29]
+def widen_kernel(plan, *refs):
+    shares, (low_result, low_input, low_neighbour) = refs[:12], refs[12:15]
+    down, up, cross_out, memory, query, self_out, self_weight, result, input_grad, neighbour_grad = refs[15:25]
+    vectors, kept = refs[25:31], refs[31]
     step = pl.program_id(0)
 
     def put(out, s, at, first, count):
@@ -1049,8 +1065,8 @@
 
     for part in range(2):
         for core in range(2):
-            rows = shares[part].shape[3]
-            out_rows = slice(part * rows, part * rows + rows)
+            tall = shares[part].shape[3]
+            out_rows = slice(part * tall, part * tall + tall)
             down[out_rows, core * (D // 2) : (core + 1) * (D // 2)] = shares[part][core, 0, 0].astype(F32)
     quarter = up.shape[1] // 4
     put(up, 2, 0, 0, quarter)
@@ -1060,14 +1076,29 @@
     put(cross_out, 5, 0, 256, D // 2)
     put(query, 6, 0, 0, D // 2)
     put(self_out, 7, 0, 0, D // 2)
-    put(self_weight, 8, 0, 0, 640)
-    put(self_weight, 9, 640, 0, 512)
+    rows = shares[8].shape[3]
+    low = low_lanes((rows, 2 * HEAD))
+
+    def block(head, spot):
+        g, slot = head // plan.slots, head % plan.slots
+        core, i = g // 2, g % 2
+        spot = i if spot is None else spot
+        s, first = (8 + slot, spot * 128) if slot < 2 else (10, spot * 128) if spot < 2 else (11, 0)
+        return shares[s][core, 0, 0, :, first : first + 128].astype(F32), i
+
+    for two in range(HEADS // 2):
+        heads = (2 * two, 2 * two + 1)
+        columns = slice(two * 128, two * 128 + 128)
+        (one, i), (other, j) = [block(head, 2) for head in heads]
+        self_weight[:, columns] = jnp.where(low, swap_lanes(one) if i else one, other if j else swap_lanes(other))
+        one, other = [block(head, None)[0] for head in heads]
+        self_weight[:, slice(D + two * 128, D + two * 128 + 128)] = jnp.where(low, one, swap_lanes(other))
+        self_weight[:, slice(2 * D + two * 128, 2 * D + two * 128 + 128)] = jnp.where(low, swap_lanes(one), other)
     result[...] = low_result[...]
     input_grad[...] = low_input[...].astype(F32)
     neighbour_grad[...] = low_neighbour[...].astype(F32)
-    rows = shares[9].shape[3]
     for core in range(2):
-        kept[core, pl.ds(pl.multiple_of(step * rows, 16), rows)] = shares[9][core, 0, 0, :, 512:].astype(F32)
+        kept[core, pl.ds(pl.multiple_of(step * rows, 16), rows)] = shares[11][core, 0, 0, :, 128:].astype(F32)
 
     @pl.when(step == 3)
     def _():
@@ -1088,7 +1119,7 @@
     outs = [pl.BlockSpec((r // 4, c), lambda i: (i, 0)) for r, c in layout]
     outs += [pl.BlockSpec((D // batch,), lambda i: (0,))] * 6
     return pl.pallas_call(
-        partial(widen_kernel, batch),
+        partial(widen_kernel, plan),
         grid=(4,),
         in_specs=ins,
         out_specs=outs,
@@ -1139,27 +1170,27 @@
 
 
 def middle_kernel(plan, batch, shares, arrival_counts, names, *refs):
-    r = dict(zip(names, refs))
+    r = SimpleNamespace(**dict(zip(names, refs)))
     takes = iter(refs[len(names) :])
     sums = [next(takes) for _ in range(EARLY)]
     arrivals = [[next(takes) for _ in range(n)] for n in arrival_counts]
     (
         up, down, active, two_normed, give_upper, two_upper, two_grad, slopes,
         stream_one, stream_two, normed_grad, summed, moved_queries, moved_grads, moved,
-        load_sems, own_sems, tile_send, tile_recv, swap_send, swap_recv, group_sems, send_sems, recv_sems,
+        load_sems, own_sems, tile_send, tile_recv, swap_send, swap_recv, group_sems, near_sems, send_sems, recv_sems,
     ) = takes
     me, group, member = plan.place()
     rows, groups = plan.rows, plan.groups
-    states = [r["state%d" % s] for s in range(EARLY)]
+    states = [getattr(r, "state%d" % s) for s in range(EARLY)]
     engine = Engine(plan, batch, shares, sums, arrivals, None, send_sems, recv_sems, None)
     partner = engine.partner
     greet(engine.peers())
     here, there = pl.ds(0, rows), pl.ds(rows, rows)
     ff = up.shape[1]
     loads = [
-        pltpu.make_async_copy(r["memory"], slopes, load_sems.at[2]),
-        pltpu.make_async_copy(r["up_weight"], up, load_sems.at[0]),
-        pltpu.make_async_copy(r["down_weight"], down, load_sems.at[1]),
+        pltpu.make_async_copy(r.memory, slopes, load_sems.at[2]),
+        pltpu.make_async_copy(r.up_weight, up, load_sems.at[0]),
+        pltpu.make_async_copy(r.down_weight, down, load_sems.at[1]),
     ]
     for copy in loads:
         copy.start()
@@ -1167,8 +1198,8 @@
     mine = pl.ds(pl.multiple_of(member * half, 128), half)
     theirs = pl.ds(pl.multiple_of((1 - member) * half, 128), half)
     grad_swap = [
-        pltpu.make_async_copy(r["cotangent"].at[:, mine], two_grad.at[here], own_sems.at[0]),
-        send(r["cotangent"].at[:, theirs], two_grad.at[there], swap_send.at[0], swap_recv.at[0], partner),
+        pltpu.make_async_copy(r.cotangent.at[:, mine], two_grad.at[here], own_sems.at[0]),
+        send(r.cotangent.at[:, theirs], two_grad.at[there], swap_send.at[0], swap_recv.at[0], partner),
     ]
     for copy in grad_swap:
         copy.start()
@@ -1184,10 +1215,10 @@
         whole = moved[...].reshape(stretches * STRETCH, D)
         return pltpu.roll(whole, stretches * STRETCH - 1, 0)[:rows]
 
-    stream_one[...] = r["tokens"][...].astype(F32) + matmul(r["context"][...], r["self_output"][...])
-    normed_two = (norm_parts(stream_one[...])[0] * as_row(r["second_gain"]) + as_row(r["second_shift"])).astype(BF16)
-    r["normed_two"][...] = normed_two
-    cross_queries = matmul(normed_two, r["query_weight"][...]).astype(BF16).astype(F32) * (HEAD ** -0.5)
+    stream_one[...] = r.tokens[...].astype(F32) + matmul(r.context[...], r.self_output[...])
+    normed_two = (norm_parts(stream_one[...])[0] * as_row(r.second_gain) + as_row(r.second_shift)).astype(BF16)
+    r.normed_two[...] = normed_two
+    cross_queries = matmul(normed_two, r.query_weight[...]).astype(BF16).astype(F32) * (HEAD ** -0.5)
     moved_queries[...] = move(cross_queries)
     loads[0].wait()
 
@@ -1200,9 +1231,9 @@
             moved[i, :, columns] = unstack_heads(matmul(chances.astype(BF16), slopes[i, :, values]))
 
     cross_low = (move_back() * keep).astype(BF16)
-    r["cross_low"][...] = cross_low
-    stream_two[...] = stream_one[...] + matmul(cross_low, r["cross_output"][...])
-    two_normed[here] = (norm_parts(stream_two[...])[0] * as_row(r["third_gain"]) + as_row(r["third_shift"])).astype(BF16)
+    r.cross_low[...] = cross_low
+    stream_two[...] = stream_one[...] + matmul(cross_low, r.cross_output[...])
+    two_normed[here] = (norm_parts(stream_two[...])[0] * as_row(r.third_gain) + as_row(r.third_shift)).astype(BF16)
     normed_swap = send(two_normed.at[here], two_normed.at[there], swap_send.at[1], swap_recv.at[1], partner)
     normed_swap.start()
     normed_grad[...] = jnp.zeros_like(normed_grad)
@@ -1227,7 +1258,7 @@
         active_low = (upper * below).astype(BF16)
         active[here, columns] = active_low
         tile_copy(t).start()
-        grad = back_product(r["cotangent"][...], down[columns])
+        grad = back_product(r.cotangent[...], down[columns])
         upper_low = (grad * (below + upper * density)).astype(BF16)
         spot = pl.ds(pl.multiple_of(lax.rem(t, tiles // 2) * tile, tile), tile)
 
@@ -1242,9 +1273,16 @@
         summed[...] += matmul(active_low, down[columns])
         normed_grad[...] += back_product(upper_low, up[:, columns])
 
+    near = down.at[pl.ds(0, stretches * SPAN)]
+    near_loads = [
+        pltpu.make_async_copy(r.edge, down.at[pl.ds(0, SPAN)], near_sems.at[0]),
+        pltpu.make_async_copy(r.neighbours, down.at[pl.ds(SPAN, (stretches - 1) * SPAN)], near_sems.at[1]),
+    ]
+    for copy in near_loads:
+        copy.start()
     upper_swap = send(give_upper, two_upper.at[there], swap_send.at[2], swap_recv.at[2], partner)
     upper_swap.start()
-    r["result"][...] = (stream_two[...] + summed[...]).astype(BF16)
+    r.result[...] = (stream_two[...] + summed[...]).astype(BF16)
 
     def fill_down(s):
         if s > 0:
@@ -1281,17 +1319,17 @@
     for run in running:
         next(run, None)
 
-    gain_grad, shift_grad, inner = norm_back(stream_two[...], as_row(r["third_gain"]), normed_grad[...])
-    r["vectors"][1:2] = gain_grad
-    r["vectors"][3:4] = shift_grad
-    stream_two_grad = r["cotangent"][...].astype(F32) + inner
+    gain_grad, shift_grad, inner = norm_back(stream_two[...], as_row(r.third_gain), normed_grad[...])
+    r.vectors[1:2] = gain_grad
+    r.vectors[3:4] = shift_grad
+    stream_two_grad = r.cotangent[...].astype(F32) + inner
     normed_grad[...] = stream_two_grad
     branch_low = stream_two_grad.astype(BF16)
-    r["branch"][...] = branch_low
-    moved_grads[...] = move(back_product(branch_low, r["cross_output"][...]) * keep)
+    r.branch[...] = branch_low
+    moved_grads[...] = move(back_product(branch_low, r.cross_output[...]) * keep)
 
     def group_copy(i):
-        return pltpu.make_async_copy(slopes.at[i], r["memory_grad"].at[i], group_sems.at[i])
+        return pltpu.make_async_copy(slopes.at[i], r.memory_grad.at[i], group_sems.at[i])
 
     @pl.loop(0, stretches)
     def _(i):
@@ -1311,27 +1349,50 @@
         group_copy(i).start()
 
     query_grad = move_back().astype(BF16)
-    r["query_grad"][...] = query_grad
+    r.query_grad[...] = query_grad
     gain_grad, shift_grad, inner = norm_back(
-        stream_one[...], as_row(r["second_gain"]), back_product(query_grad, r["query_weight"][...])
-    )
-    r["vectors"][0:1] = gain_grad
-    r["vectors"][2:3] = shift_grad
-    r["vectors"][4:8] = jnp.zeros((4, D), F32)
+        stream_one[...], as_row(r.second_gain), back_product(query_grad, r.query_weight[...])
+    )
+    r.vectors[0:1] = gain_grad
+    r.vectors[2:3] = shift_grad
+    r.vectors[4:8] = jnp.zeros((4, D), F32)
     stream_one_grad = normed_grad[...] + inner
-    r["stream_grad"][...] = stream_one_grad
+    r.stream_grad[...] = stream_one_grad
     self_low = stream_one_grad.astype(BF16)
-    r["self_low"][...] = self_low
-    r["grad_out"][...] = back_product(self_low, r["self_output"][...]).astype(BF16)
+    r.self_low[...] = self_low
+    grad_out = back_product(self_low, r.self_output[...]).astype(BF16).astype(F32)
+
+    for head in range(HEADS):
+        block = (head // 2) * 128
+        r.packed_grads[head] = pack_rows(grad_out[:, block : block + 128], head).astype(BF16)
+
+    for copy in near_loads:
+        copy.wait()
+    span_rows = stretches * SPAN
+
+    def memory_tile(owner, t):
+        columns = pl.ds(pl.multiple_of(owner * D + t * 256, 256), 256)
+        return outer_sum(near[...], slopes[:, :, columns].reshape(span_rows, 256)).astype(BF16)
+
+    for t in range(D // 256):
+        up[:, t * 256 : t * 256 + 256] = memory_tile(1 - member, t)
+    memory_swap = send(
+        up.at[:, pl.ds(0, D)], up.at[:, pl.ds(D, D)], swap_send.at[3], swap_recv.at[3], partner
+    )
+    memory_swap.start()
+    for t in range(D // 256):
+        up[:, 2 * D + t * 256 : 2 * D + t * 256 + 256] = memory_tile(member, t)
     for run in running:
         next(run, None)
+    memory_swap.wait()
+    r.memory_part[...] = add(up[:, 2 * D : 3 * D], up[:, D : 2 * D])
 
     @pl.loop(0, stretches)
     def _(i):
         group_copy(i).wait()
 
 
-def middle(plan, batch, tokens, context, self_output, second_gain, second_shift, third_gain, third_shift, query_weight, memory, cross_output, up_weight, down_weight, cotangent):
+def middle(plan, batch, tokens, context, self_output, second_gain, second_shift, third_gain, third_shift, query_weight, memory, neighbours, edge, cross_output, up_weight, down_weight, cotangent):
     rows = plan.rows
     ff = up_weight.shape[1]
     stretches = memory.shape[0]
@@ -1343,17 +1404,18 @@
         cross_output=cross_output, cotangent=cotangent,
     )
     near = len(inputs)
-    inputs.update(memory=memory, up_weight=up_weight, down_weight=down_weight)
+    inputs.update(memory=memory, up_weight=up_weight, down_weight=down_weight, neighbours=neighbours, edge=edge)
     low = ((rows, D), BF16)
     outputs = dict(
-        result=low, normed_two=low, cross_low=low, branch=low, query_grad=low, self_low=low, grad_out=low,
+        result=low, normed_two=low, cross_low=low, branch=low, query_grad=low, self_low=low,
+        packed_grads=((HEADS, rows // 2, 128), BF16), memory_part=((D, D), BF16),
         stream_grad=((rows, D), F32), vectors=((8, D), F32),
     )
     steps = [step_shapes(shares[s], batch, "zyx", shares[s].order[:1]) for s in range(EARLY)]
     for s in range(EARLY):
         outputs["state%d" % s] = (part_shape(shares[s], batch, "zyx".replace(shares[s].order[0], "")), BF16)
     far = len(outputs)
-    outputs["memory_grad"] = (memory.shape, BF16)
+    outputs.update(memory_grad=(memory.shape, BF16))
     scratch = [VM(part_shape(shares[s], batch, "zyx"), BF16) for s in range(EARLY)]
     scratch += [VM(shape, BF16) for shapes in steps for shape in shapes]
     scratch += [
@@ -1376,9 +1438,10 @@
         dma((1,)),
         dma((ff // 512,)),
         dma((ff // 512,)),
-        dma((3,)),
-        dma((3,)),
+        dma((4,)),
+        dma((4,)),
         dma((stretches,)),
+        dma((2,)),
         dma((EARLY, batch - 1)),
         dma((EARLY, batch - 1)),
     ]
@@ -1394,7 +1457,7 @@
         ),
         name="middle",
     )(*inputs.values())
-    return dict(zip(outputs, out))
+    return SimpleNamespace(**dict(zip(outputs, out)))
 
 
 def on_device(devices, batch, tokens, segment_ids, neighbours, first_gain, first_shift, self_weight, self_output, second_gain,
@@ -1405,37 +1468,36 @@
     stretch_count = neighbours.shape[1]
     ff = up_weight.shape[1]
     neighbour_rows = neighbours[0].reshape(stretch_count * SPAN, D)
-    normed_one, logs, starts, context, edge, queries, pairs, outs, memory = attend(
+    normed_one, logs, starts, context, edge, queries, pairs, outs, memory, packed = attend(
         plan, tokens[0], first_gain, first_shift, segment_ids, self_weight, neighbour_rows, memory_weight
     )
     mid = middle(
         plan, batch, tokens[0], context, self_output, second_gain, second_shift, third_gain, third_shift, query_weight,
-        memory, cross_output, up_weight, down_weight, cotangent[0],
+        memory, neighbour_rows, edge, cross_output, up_weight, down_weight, cotangent[0],
     )
     input_grad, neighbour_grad, shares = tail(
         plan,
         batch,
-        mid["grad_out"],
+        mid.packed_grads,
         queries,
         pairs,
         outs,
         logs,
         starts,
-        [mid["cross_low"], mid["normed_two"], context, normed_one],
-        [mid["branch"], mid["query_grad"], mid["self_low"]],
-        [mid["state%d" % s] for s in range(EARLY)],
-        neighbour_rows,
-        edge,
-        mid["memory_grad"].reshape((stretch_count + 1) * SPAN, 2 * D),
+        [mid.cross_low, mid.normed_two, context, normed_one],
+        [mid.branch, mid.query_grad, mid.self_low],
+        [getattr(mid, "state%d" % s) for s in range(EARLY)],
+        mid.memory_part.reshape(batch, 2, 2, D // (batch * 4), D),
+        mid.memory_grad.reshape((stretch_count + 1) * SPAN, 2 * D),
         memory_weight,
-        self_weight,
+        packed,
         tokens[0],
         first_gain,
-        mid["stream_grad"],
-        mid["vectors"],
+        mid.stream_grad,
+        mid.vectors,
         ff,
     )
-    wide = widen(plan, batch, ff, shares, mid["result"], input_grad, neighbour_grad)
+    wide = widen(plan, batch, ff, shares, mid.result, input_grad, neighbour_grad)
     down, up, cross_out, memory_w, query, self_out, self_w, result, input_grad, neighbour_grad = wide[:10]
     vector = wide[10:]
     return (

time: 261 us -> 248 us (0.950)
  Pallas kernels: 257 us -> 243 us
    pallas_call x1, Pallas kernels: 134 us -> 119 us  [tail(): pl.pallas_call(partial(tail_kernel, plan, batch, shares, [len(s) for s in...]
where the time goes in v1:
time: 248 us; the launch traced here: 244 us
  Pallas kernels  243 us (98%)
    pallas_call x1, Pallas kernels, tail(): pl.pallas_call(partial(tail_kernel, plan, batch, shares, [len(s) for s in...  119 us
    pallas_call x1, Pallas kernels, middle(): pl.pallas_call(partial(middle_kernel, plan, batch, shares, [len(s) for s...  65.1 us
    pallas_call x1, Pallas kernels, attend(): pl.pallas_call(partial(attend_kernel, plan), out_shape=[jax.ShapeDtypeStr...  49.2 us
    pallas_call x1, Pallas kernels, widen(): pl.pallas_call(partial(widen_kernel, plan), grid=(4,), in_specs=ins, out_...  9.87 us

profile of v1, /device:TPU:0, one launch (start us, length us, event | category | flops | bytes accessed | tf_op | source)
XLA Modules:
  0.0 243.7 jit_solution(7793360929240444792)
XLA Ops:
  0.6 49.2 %attend.1 = (bf16[384,768]{1,0:T(8,128)(2,1)}, f32[3,4,8,384]{3,2,1,0:T(8,128)}, s32[4,8,384]{2,1,0:T(8,128)}, bf16[384,768]{1,0:T(8,128)(2,1)}, bf16[256,768]{1...) custom-call(bf16[384,768]{1,0:T(8,128)(2,1)} %bitcast.11, ...), custom_call_target="tpu_custom_call" | custom-call | tf_op jit(solution)/shard_map/attend/pallas_call | solution.py:400
  49.8 65.1 %middle.1 = (bf16[384,768]{1,0:T(8,128)(2,1)}, bf16[384,768]{1,0:T(8,128)(2,1)}, bf16[384,768]{1,0:T(8,128)(2,1)}, bf16[384,768]{1,0:T(8,128)(2,1)}, bf16[384,76...) custom-call(bf16[384,768]{1,0:T(8,128)(2,1)} %bitcast.12, ...), custom_call_target="tpu_custom_call" | custom-call | tf_op jit(solution)/shard_map/middle/pallas_call | solution.py:1449
  114.9 118.7 %tail.1 = (bf16[384,768]{1,0:T(8,128)(2,1)}, bf16[1536,768]{1,0:T(8,128)(2,1)}, bf16[2,2,2,96,384]{4,3,2,1,0:T(8,128)(2,1)}, bf16[2,2,2,96,384]{4,3,2,1,0:T(8,12...) custom-call(bf16[12,192,128]{2,1,0:T(8,128)(2,1)} %get-tuple-element, ...), custom_call_target="tpu_custom_call" | custom-call | tf_op jit(solution)/shard_map/tail/pallas_call | solution.py:1039
  233.7 9.9 %widen.1 = (f32[768,768]{1,0:T(8,128)}, f32[192,3072]{1,0:T(8,128)}, f32[192,768]{1,0:T(8,128)}, f32[192,1536]{1,0:T(8,128)}, f32[192,768]{1,0:T(8,128)}, /*inde...) custom-call(bf16[2,2,2,96,384]{4,3,2,1,0:T(8,128)(2,1)} %get-tuple-e, ...), custom_call_target="tpu_custom_call" | custom-call | tf_op jit(solution)/shard_map/widen/pallas_call | solution.py:1121

commit v2 on v1

--- a/solution.py
+++ b/solution.py
@@ -451,28 +451,33 @@
     short, tall = D // (batch * groups), ff // (batch * groups * 2)
     half = D // 2
     return [
-        Share(tall, half, "xzy", []),
+        Share(tall, half, "xyz", []),
         Share(tall, half, "yxz", []),
-        Share(short, ff // 4, "xzy", [Product(0, 0, ff // 4)]),
+        Share(short, ff // 4, "xyz", [Product(0, 0, ff // 4)]),
         Share(short, ff // 4, "zyx", [Product(0, ff // 4, ff // 4)]),
-        Share(short, 512, "xyz", []),
-        Share(short, 256 + half, "yxz", [Product(0, 0, half, 256)]),
-        Share(short, half, "yzx", [Product(1, 0, half)]),
-        Share(short, half, "zyx", [Product(2, 0, half)]),
-        Share(short, half, "xyz", [Product(3, 0, half)]),
-        Share(short, half, "zyx", [Product(4, 0, half)]),
-        Share(short, 256, "xzy", [Product(5, 0, 256)]),
-        Share(short, 256, "yxz", [Product(5, 256, 128)], vectors=128),
+        Share(short, 512, "zyx", []),
+        Share(short, 256 + half, "xzy", [Product(0, 0, half, 256)]),
+        Share(short, half, "yxz", [Product(1, 0, half)]),
+        Share(short, half, "xzy", [Product(2, 0, half)]),
+        Share(short, half, "yzx", [Product(3, 0, half)]),
+        Share(short, half, "xzy", [Product(4, 0, half)]),
+        Share(short, 256, "yxz", [Product(5, 0, 256)]),
+        Share(short, 256, "yzx", [Product(5, 256, 128)], vectors=128),
     ]
 
 
-EARLY = 4
+EARLY_STEPS = (2, 2, 1, 1)
+EARLY = len(EARLY_STEPS)
+
+
+def axes_after(share, steps):
+    return "".join(axis for axis in "zyx" if axis not in share.order[:steps])
 
 SCHEDULE = (
-    (), (), (), (), (), (), (-1, 5, 4, 3), (8,), (1, 6), (0, 2), (-2, 8, 0, 3), (9, 5, 1, 2), (),
-    (7, 0, 1, 2), (10, 4, 3), (11, 1), (5, 0), (8, 2, 3, 1), (9, 6, 7, 0), (10, 11, 4, 5, 2, 3), (9, 6, 8),
-    (11, 7, 4), (9,), (10,), (6,), (8,), (5,), (7,), (11,), (10,), (5,), (9,), (6,), (10,), (11,), (4,), (8,),
-    (7,), (6,), (9,), (4,), (10,), (11,), (7,), (8,), (9,), (10,), (11,),
+    (), (), (), (), (0,), (6, 1), (), (7,), (1, 2), (4,), (7, 5), (-1, 2, -2, 6, 8), (9, 3), (),
+    (8, 0, 5, 10), (4, 11, 9), (4,), (2, 3), (), (1,), (), (7, 6), (5, 10, 11, 3, 8), (4, 7), (0, 6, 8), (),
+    (), (9, 10), (5,), (2, 11, 9, 11), (6,), (10, 8), (4, 9, 11), (2, 3, 5, 4, 10), (6, 8, 7), (11,),
+    (5, 9, 1, 10), (7,), (8, 11, 3, 9, 0, 10),
 )
 
 
@@ -552,7 +557,7 @@
                     value = value + arrived[i].astype(F32)
             else:
                 value = value + arrived[...].astype(F32)
-            if stop is None:
+            if stop is None or number < len(order) - 1:
                 total[spot] = value.astype(BF16)
             else:
                 stop[...] = value.astype(BF16)
@@ -782,8 +787,8 @@
     running = []
     for s, share in enumerate(shares):
         if s < EARLY:
-            axes = "zyx".replace(share.order[0], "")
-            running.append(engine.steps(s, partial(ready, s), axes, share.order[1:]))
+            axes = axes_after(share, EARLY_STEPS[s])
+            running.append(engine.steps(s, partial(ready, s), axes, share.order[EARLY_STEPS[s] :]))
         else:
             running.append(engine.steps(s, partial(fill, s), "zyx", share.order))
 
@@ -982,8 +987,9 @@
     inputs.update({"state%d" % m: state for m, state in enumerate(states)})
     inputs.update(memory_part=memory_part, memory_grad=memory_grad, memory_weight=memory_weight)
     widths = [right.shape[1] // 2 for right in rights] + [D // 2] * slots
-    axes = ["zyx".replace(s.order[0], "") if n < EARLY else "zyx" for n, s in enumerate(shares)]
-    orders = [s.order[1:] if n < EARLY else s.order for n, s in enumerate(shares)]
+    early = EARLY_STEPS + (0,) * (len(shares) - EARLY)
+    axes = [axes_after(share, count) for share, count in zip(shares, early)]
+    orders = [share.order[count:] for share, count in zip(shares, early)]
     steps = [step_shapes(share, batch, axes[n], orders[n]) for n, share in enumerate(shares)]
     scratch = [VM((2 * rows, left.shape[1]), BF16) for left in lefts]
     scratch += [VM((2 * rows, width), BF16) for width in widths]
@@ -1314,7 +1320,8 @@
 
     fills = [fill_down, fill_down, fill_up, fill_up]
     running = [
-        engine.steps(s, partial(fills[s], s), "zyx", shares[s].order[:1], states[s]) for s in range(EARLY)
+        engine.steps(s, partial(fills[s], s), "zyx", shares[s].order[: EARLY_STEPS[s]], states[s])
+        for s in range(EARLY)
     ]
     for run in running:
         next(run, None)
@@ -1348,6 +1355,8 @@
             slopes[i, :, values] = outer_sum(chances.astype(BF16), stacked_grad).astype(BF16)
         group_copy(i).start()
 
+    for run in running[:2]:
+        next(run, None)
     query_grad = move_back().astype(BF16)
     r.query_grad[...] = query_grad
     gain_grad, shift_grad, inner = norm_back(
@@ -1411,9 +1420,9 @@
         packed_grads=((HEADS, rows // 2, 128), BF16), memory_part=((D, D), BF16),
         stream_grad=((rows, D), F32), vectors=((8, D), F32),
     )
-    steps = [step_shapes(shares[s], batch, "zyx", shares[s].order[:1]) for s in range(EARLY)]
+    steps = [step_shapes(shares[s], batch, "zyx", shares[s].order[: EARLY_STEPS[s]]) for s in range(EARLY)]
     for s in range(EARLY):
-        outputs["state%d" % s] = (part_shape(shares[s], batch, "zyx".replace(shares[s].order[0], "")), BF16)
+        outputs["state%d" % s] = (part_shape(shares[s], batch, axes_after(shares[s], EARLY_STEPS[s])), BF16)
     far = len(outputs)
     outputs.update(memory_grad=(memory.shape, BF16))
     scratch = [VM(part_shape(shares[s], batch, "zyx"), BF16) for s in range(EARLY)]

time: 248 us -> 242 us (0.976)
  Pallas kernels: 243 us -> 237 us
    pallas_call x1, Pallas kernels: 119 us -> 107 us  [tail(): pl.pallas_call(partial(tail_kernel, plan, batch, shares, [len(s) for s in...]
    pallas_call x1, Pallas kernels: 65.1 us -> 71.1 us  [middle(): pl.pallas_call(partial(middle_kernel, plan, batch, shares, [len(s) for s...]
where the time goes in v2:
time: 242 us; the launch traced here: 238 us
  Pallas kernels  237 us (98%)
    pallas_call x1, Pallas kernels, tail(): pl.pallas_call(partial(tail_kernel, plan, batch, shares, [len(s) for s in...  107 us
    pallas_call x1, Pallas kernels, middle(): pl.pallas_call(partial(middle_kernel, plan, batch, shares, [len(s) for s...  71.1 us
    pallas_call x1, Pallas kernels, attend(): pl.pallas_call(partial(attend_kernel, plan), out_shape=[jax.ShapeDtypeStr...  49.1 us
    pallas_call x1, Pallas kernels, widen(): pl.pallas_call(partial(widen_kernel, plan), grid=(4,), in_specs=ins, out_...  9.87 us

profile of v2, /device:TPU:0, one launch (start us, length us, event | category | flops | bytes accessed | tf_op | source)
XLA Modules:
  0.0 237.6 jit_solution(6288623185949471654)
XLA Ops:
  0.6 49.1 %attend.1 = (bf16[384,768]{1,0:T(8,128)(2,1)}, f32[3,4,8,384]{3,2,1,0:T(8,128)}, s32[4,8,384]{2,1,0:T(8,128)}, bf16[384,768]{1,0:T(8,128)(2,1)}, bf16[256,768]{1...) custom-call(bf16[384,768]{1,0:T(8,128)(2,1)} %bitcast.11, ...), custom_call_target="tpu_custom_call" | custom-call | tf_op jit(solution)/shard_map/attend/pallas_call | solution.py:400
  49.8 71.1 %middle.1 = (bf16[384,768]{1,0:T(8,128)(2,1)}, bf16[384,768]{1,0:T(8,128)(2,1)}, bf16[384,768]{1,0:T(8,128)(2,1)}, bf16[384,768]{1,0:T(8,128)(2,1)}, bf16[384,76...) custom-call(bf16[384,768]{1,0:T(8,128)(2,1)} %bitcast.12, ...), custom_call_target="tpu_custom_call" | custom-call | tf_op jit(solution)/shard_map/middle/pallas_call | solution.py:1458
  120.9 106.6 %tail.1 = (bf16[384,768]{1,0:T(8,128)(2,1)}, bf16[1536,768]{1,0:T(8,128)(2,1)}, bf16[2,2,2,96,384]{4,3,2,1,0:T(8,128)(2,1)}, bf16[2,2,2,96,384]{4,3,2,1,0:T(8,12...) custom-call(bf16[12,192,128]{2,1,0:T(8,128)(2,1)} %get-tuple-element, ...), custom_call_target="tpu_custom_call" | custom-call | tf_op jit(solution)/shard_map/tail/pallas_call | solution.py:1045
  227.5 9.9 %widen.1 = (f32[768,768]{1,0:T(8,128)}, f32[192,3072]{1,0:T(8,128)}, f32[192,768]{1,0:T(8,128)}, f32[192,1536]{1,0:T(8,128)}, f32[192,768]{1,0:T(8,128)}, /*inde...) custom-call(bf16[2,2,2,96,384]{4,3,2,1,0:T(8,128)(2,1)} %get-tuple-e, ...), custom_call_target="tpu_custom_call" | custom-call | tf_op jit(solution)/shard_map/widen/pallas_call | solution.py:1127
